TPU v7x, 32 devices: a whole 2x2x4 slice. The times are simulated.
32 devices in a mesh: row: 8 (over z, core), col: 4 (over y, x).
Axes of the slice: x: 2, y: 2, z: 4, core: 2. Of those that a mesh axis runs over, the one named last changes fastest.
Arguments:
- work: float32 [4096, 2048], P('row', 'col'), may hold values from -6 to 6
- a_tiles: bfloat16 [8, 8, 512, 512], P('row', None, 'col'), may hold values from -0.078125 to 0.078125
- b_tiles: bfloat16 [4, 4, 512, 512], P(None, 'col', 'row'), may hold values from -0.078125 to 0.078125
- u_powers: float32 [8, 3, 512, 512], P('row', None, 'col'), may hold values from -1 to 1, as said below
- v_powers: float32 [4, 3, 512, 512], P('col', None, 'row'), may hold values from -1 to 1, as said below
- shift: float32 [1], replicated, may hold values from 0.5 to 2
Outputs:
- progress: float32 [4096, 2048], P('row', 'col')
Inputs may be any that keep to these rules, and one draw needn't show every extreme that they name: u_powers[i] holds U, U^2 and U^4 for a lower triangular U whose diagonal entries have magnitudes 0.3 to 0.9. v_powers[j] holds V, V^2 and V^4 for an upper triangular V whose diagonal entries have magnitudes 0.3 to 0.9.
All inputs are finite; a program needn't handle non-finite values.
Results may differ from a plain program's by a relative error of at most 0.0023.
Values may be sent and summed in bfloat16 or wider, within the bound.
A program may use at most 128 MiB of HBM per device.

v0:
```python
import jax
import jax.numpy as jnp
import numpy as np
from jax import lax
from jax.sharding import PartitionSpec as P

FRONTS = 3


finest = lax.Precision.HIGHEST


def from_root(array, axis, root):
    mine = lax.axis_index(axis) == root
    return lax.psum(jnp.where(mine, array, jnp.zeros_like(array)), axis)


def product(left_side, right_side):
    return jnp.dot(left_side, right_side, preferred_element_type=jnp.float32, precision=finest)


def keep(source):
    return source


def per_device(work, a_tiles, b_tiles, u_powers, v_powers, shift):
    rows_count = lax.axis_size("row")
    cols_count = lax.axis_size("col")
    my_row = lax.axis_index("row")
    my_col = lax.axis_index("col")
    my_front = my_row + my_col
    first = max(0, (rows_count + cols_count) // 2 - FRONTS)
    width = work.shape[0]
    identity = jnp.eye(width, dtype=jnp.float32)
    shift_value = shift[0]
    u_stack = lax.all_gather(u_powers, "col", axis=2, tiled=True)[0]
    v_stack = lax.all_gather(v_powers, "row", axis=2, tiled=True)[0]

    def powers_of():
        return ([u_stack[power] for power in range(3)], [v_stack[power] for power in range(3)])

    def solve(source):
        u_list, v_list = powers_of()
        current = product(product(identity - u_list[0], source), identity - v_list[0]) / (
            2.0 * shift_value
        )
        for power in range(3):
            current = current + product(product(u_list[power], current), v_list[power])
        return current

    current = work
    for number in range(FRONTS):
        front = first + number
        current = lax.cond(my_front == front, solve, keep, current)
        sent = current.astype(jnp.bfloat16)
        down_row = front - my_col
        across_col = front - my_row
        valid_down = (down_row >= 0) & (down_row < rows_count)
        valid_across = (across_col >= 0) & (across_col < cols_count)
        down_clip = jnp.clip(down_row, 0, rows_count - 1)
        across_clip = jnp.clip(across_col, 0, cols_count - 1)
        down_tile = from_root(sent, "row", down_clip)
        across_tile = from_root(sent, "col", across_clip)
        a_rows = np.clip(front - np.arange(cols_count), 0, rows_count - 1).astype(np.int32)
        b_rows = np.clip(front - np.arange(rows_count), 0, cols_count - 1).astype(np.int32)
        a_tile = lax.all_to_all(
            a_tiles[0, a_rows], "col", split_axis=0, concat_axis=0, tiled=True
        ).reshape(width, width)
        b_tile = lax.all_to_all(
            b_tiles[b_rows, 0], "row", split_axis=0, concat_axis=0, tiled=True
        ).reshape(width, width)

        def update(source):
            minus_a = jnp.dot(a_tile, down_tile, preferred_element_type=jnp.float32)
            minus_b = jnp.dot(across_tile, b_tile, preferred_element_type=jnp.float32)
            return (
                source - jnp.where(valid_down, minus_a, 0.0) - jnp.where(valid_across, minus_b, 0.0)
            )

        current = lax.cond(my_front > front, update, keep, current)
    return current


def solution(mesh):
    placed = (
        P("row", "col"),
        P("row", None, "col", None),
        P(None, "col", "row", None),
        P("row", None, "col", None),
        P("col", None, "row", None),
        P(),
    )
    return jax.shard_map(
        per_device, mesh=mesh, in_specs=placed, out_specs=P("row", "col"), check_vma=False
    )
```

profile of v0, /device:TPU:24, one launch (start us, length us, event | category | flops | bytes accessed | tf_op | source)
XLA Modules:
  0.0 521.4 jit_solution(9968293450889859236)
XLA Ops:
  6.5 0.0 copy-start
  6.6 0.0 copy-start.15
  6.6 0.7 all-gather.3.cloned.1.call-update
  7.3 0.0 all-gather.5.cloned.1.call-start
  7.3 0.7 all-gather.5.cloned.1.call-update
  8.0 1.4 gather_fusion
  9.4 3.8 all-to-all-start
  13.3 0.0 copy-done.18
  13.3 1.4 gather_fusion.2
  14.6 8.0 %all-to-all-done = bf16[4,128,512]{2,1,0:T(8,128)(2,1)S(1)} async-done(((bf16[4,128,512]{2,1,0:T(8,128)(2,1)}), bf16[4,128,512]{2,1,0:T(8,128)(2,1)S(1)}, u32[]{:S(2)}, u32[]{:S(2)}) %all-to-all-start) | async-done | bytes 524320 | tf_op jit(solution)/shard_map/all_to_all | solution.py:66
  22.7 0.8 copy-done.11
  23.5 3.5 all-to-all-start.2
  27.0 1.4 gather_fusion.1
  28.4 6.9 %all-to-all-done.2 = bf16[4,128,512]{2,1,0:T(8,128)(2,1)S(1)} async-done(((bf16[4,128,512]{2,1,0:T(8,128)(2,1)}), bf16[4,128,512]{2,1,0:T(8,128)(2,1)S(1)}, u32[]{:S(2)}, u32[]{:S(2)}) %all-to-all-start.2) | async-done | bytes 524320 | tf_op jit(solution)/shard_map/all_to_all | solution.py:66
  35.3 5.1 all-to-all-start.1
  40.4 0.1 fusion.60
  40.6 17.1 %all-gather.3.cloned.1.call-done = f32[1,3,512,512]{3,2,1,0:T(8,128)} async-done(((f32[1,3,128,512]{3,2,1,0:T(8,128)}), f32[1,3,512,512]{3,2,1,0:T(8,128)}) %all-gather.3.cloned.1.call-update) | async-done | bytes 3145744 | tf_op jit(solution)/shard_map/all_gather | solution.py:36
  57.7 37.9 %all-gather.5.cloned.1.call-done = f32[1,3,512,512]{3,2,1,0:T(8,128)} async-done(((f32[1,3,64,512]{3,2,1,0:T(8,128)}), f32[1,3,512,512]{3,2,1,0:T(8,128)}) %all-gather.5.cloned.1.call-update) | async-done | bytes 3145744 | tf_op jit(solution)/shard_map/all_gather | solution.py:37
  95.6 9.6 %conditional.6 = (f32[512,512]{1,0:T(8,128)S(1)}) conditional(s32[]{:T(128)} %convert_element_type.45, f32[512,512]{1,0:T(8,128)S(1)} %copy-done.2, (f32[3,512,512]{2,1,0:T(8,128)}, f32[512,512]{1,0:T(8,128)S(1)}, f32[512,512]{1,0:T(8,128)S(1)}, f32[3,512,512]{2,1,0:T(8,128)}, f32[512,512]{1,0:T(8,128)S(1)}, /*index=5*/f32[]{:T(128)}) %tuple.90), branch_computations={%region_0.0_spmd, %region_1.0_spmd} | conditional | flops 12886474752 | bytes 55574608 | solution.py:54
  105.2 0.0 copy-start.14
  105.2 1.0 broadcast_select_fusion.4
  106.2 0.0 all-reduce.13.cloned.1.call-update
  106.2 0.0 all-reduce.15.cloned.1.call-start
  106.3 0.5 all-reduce.15.cloned.1.call-update
  106.8 1.4 gather_fusion.3
  108.3 0.0 all-to-all-done.1
  108.3 21.4 %all-to-all-start.3 = ((bf16[8,64,512]{2,1,0:T(8,128)(2,1)}), bf16[8,64,512]{2,1,0:T(8,128)(2,1)}, u32[]{:S(2)}, u32[]{:S(2)}) async-start(bf16[8,64,512]{2,1,0:T(8,128)(2,1)} %gather_fusion.3), calls=%async_computation.3 | async-start | bytes 1048576 | tf_op jit(solution)/shard_map/all_to_all | solution.py:69
  129.6 53.8 %all-reduce.13.cloned.1.call-done = bf16[512,512]{1,0:T(8,128)(2,1)} async-done(((bf16[512,512]{1,0:T(8,128)(2,1)}), bf16[512,512]{1,0:T(8,128)(2,1)}) %all-reduce.13.cloned.1.call-update) | async-done | bytes 524304 | tf_op jit(solution)/shard_map/psum | solution.py:15
  183.5 49.5 %all-reduce.15.cloned.1.call-done = bf16[512,512]{1,0:T(8,128)(2,1)} async-done(((bf16[512,512]{1,0:T(8,128)(2,1)}), bf16[512,512]{1,0:T(8,128)(2,1)}) %all-reduce.15.cloned.1.call-update) | async-done | bytes 524304 | tf_op jit(solution)/shard_map/psum | solution.py:15
  232.9 4.8 conditional.7
  232.9 2.6 convolution_select_fusion.2
  235.5 2.2 fusion.57
  237.7 9.4 %conditional.8 = (f32[512,512]{1,0:T(8,128)S(1)}) conditional(s32[]{:T(128)} %convert_element_type.43, f32[512,512]{1,0:T(8,128)S(1)} %get-tuple-element.270, (f32[3,512,512]{2,1,0:T(8,128)}, f32[512,512]{1,0:T(8,128)S(1)}, f32[512,512]{1,0:T(8,128)S(1)}, f32[3,512,512]{2,1,0:T(8,128)}, f32[512,512]{1,0:T(8,128)S(1)}, /*index=5*/f32[]{:T(128)}) %tuple.91), branch_computations={%region_6.7_spmd, %region_7.8_spmd} | conditional | flops 12886474752 | bytes 55574608 | solution.py:54
  247.1 0.0 copy-start.16
  247.1 0.0 copy-start.13
  247.1 1.0 broadcast_select_fusion.2
  248.2 0.0 all-reduce.17.cloned.1.call-update
  248.2 0.0 all-reduce.19.cloned.1.call-start
  248.2 0.5 all-reduce.19.cloned.1.call-update
  248.8 1.4 gather_fusion.4
  250.2 0.0 all-to-all-done.3
  250.2 4.2 all-to-all-start.4
  254.4 1.4 gather_fusion.5
  255.8 62.0 %all-reduce.17.cloned.1.call-done = bf16[512,512]{1,0:T(8,128)(2,1)} async-done(((bf16[512,512]{1,0:T(8,128)(2,1)}), bf16[512,512]{1,0:T(8,128)(2,1)}) %all-reduce.17.cloned.1.call-update) | async-done | bytes 524304 | tf_op jit(solution)/shard_map/psum | solution.py:15
  317.8 49.2 %all-reduce.19.cloned.1.call-done = bf16[512,512]{1,0:T(8,128)(2,1)} async-done(((bf16[512,512]{1,0:T(8,128)(2,1)}), bf16[512,512]{1,0:T(8,128)(2,1)}) %all-reduce.19.cloned.1.call-update) | async-done | bytes 524304 | tf_op jit(solution)/shard_map/psum | solution.py:15
  367.0 4.8 conditional.9
  367.0 2.6 convolution_select_fusion.4
  369.6 2.2 fusion.59
  371.8 1.8 conditional.10
  373.7 0.0 all-to-all-done.4
  373.7 26.5 %all-to-all-start.5 = ((bf16[8,64,512]{2,1,0:T(8,128)(2,1)}), bf16[8,64,512]{2,1,0:T(8,128)(2,1)S(1)}, u32[]{:S(2)}, u32[]{:S(2)}) async-start(bf16[8,64,512]{2,1,0:T(8,128)(2,1)} %gather_fusion.5), calls=%async_computation.5 | async-start | bytes 1048576 | tf_op jit(solution)/shard_map/all_to_all | solution.py:69
  400.1 1.1 broadcast_select_fusion
  401.2 0.0 all-reduce.21.cloned.1.call-update
  401.2 0.0 all-reduce.23.cloned.1.call-start
  401.3 0.7 all-reduce.23.cloned.1.call-update
  402.0 11.7 %all-to-all-done.5 = bf16[8,64,512]{2,1,0:T(8,128)(2,1)S(1)} async-done(((bf16[8,64,512]{2,1,0:T(8,128)(2,1)}), bf16[8,64,512]{2,1,0:T(8,128)(2,1)S(1)}, u32[]{:S(2)}, u32[]{:S(2)}) %all-to-all-start.5) | async-done | bytes 524320 | tf_op jit(solution)/shard_map/all_to_all | solution.py:69
  413.7 45.5 %all-reduce.21.cloned.1.call-done = bf16[512,512]{1,0:T(8,128)(2,1)} async-done(((bf16[512,512]{1,0:T(8,128)(2,1)}), bf16[512,512]{1,0:T(8,128)(2,1)}) %all-reduce.21.cloned.1.call-update) | async-done | bytes 524304 | tf_op jit(solution)/shard_map/psum | solution.py:15
  459.2 49.6 %all-reduce.23.cloned.1.call-done = bf16[512,512]{1,0:T(8,128)(2,1)} async-done(((bf16[512,512]{1,0:T(8,128)(2,1)}), bf16[512,512]{1,0:T(8,128)(2,1)}) %all-reduce.23.cloned.1.call-update) | async-done | bytes 524304 | tf_op jit(solution)/shard_map/psum | solution.py:15
  508.8 4.3 conditional.11
  508.8 0.8 copy-done.12
  509.6 1.6 convolution_select_fusion
  511.2 1.8 fusion.55
  513.0 0.0 copy-start.1
  513.1 1.0 copy-done.1
  (20 shorter events, 0.0 us)
Async XLA Ops:
  6.5 1.5 copy-start
  6.5 1.5 copy-start.17
  6.5 6.7 %copy-start.18 = (s32[4]{0:T(128)S(1)}, s32[4]{0:T(128)}, u32[]{:S(2)}) copy-start(s32[4]{0:T(128)} %constant.195) | copy-start | bytes 52
  6.5 51.1 %all-gather.3.cloned.1.call-start = ((), (), s32[]{:S(2)}) async-start(), calls=%async_computation.6 | async-start | bytes 3932160 | tf_op jit(solution)/shard_map/all_gather | solution.py:36
  6.5 20.4 %copy-start.9 = (bf16[4,1,64,512]{3,2,1,0:T(8,128)(2,1)S(1)}, bf16[4,1,64,512]{3,2,1,0:T(8,128)(2,1)}, u32[]{:S(2)}) copy-start(bf16[4,1,64,512]{3,2,1,0:T(8,128)(2,1)} %param.32) | copy-start | bytes 786436
  6.6 20.4 %copy-start.15 = (s32[8]{0:T(128)S(1)}, s32[8]{0:T(128)}, u32[]{:S(2)}) copy-start(s32[8]{0:T(128)} %constant.187) | copy-start | bytes 100
  7.3 88.3 %all-gather.5.cloned.1.call-start = ((), (), s32[]{:S(2)}) async-start(), calls=%async_computation.7 | async-start | bytes 3538944 | tf_op jit(solution)/shard_map/all_gather | solution.py:37
  9.4 86.2 %copy-start.2 = (f32[512,512]{1,0:T(8,128)S(1)}, f32[512,512]{1,0:T(8,128)}, u32[]{:S(2)}) copy-start(f32[512,512]{1,0:T(8,128)} %param.30) | copy-start | bytes 3145732
  9.4 13.3 %all-to-all-start = ((bf16[4,128,512]{2,1,0:T(8,128)(2,1)}), bf16[4,128,512]{2,1,0:T(8,128)(2,1)S(1)}, u32[]{:S(2)}, u32[]{:S(2)}) async-start(bf16[4,128,512]{2,1,0:T(8,128)(2,1)} %gather_fusion), calls=%async_computation | async-start | bytes 1048576 | tf_op jit(solution)/shard_map/all_to_all | solution.py:66
  22.7 0.8 copy-start.11
  23.5 11.8 %all-to-all-start.2 = ((bf16[4,128,512]{2,1,0:T(8,128)(2,1)}), bf16[4,128,512]{2,1,0:T(8,128)(2,1)S(1)}, u32[]{:S(2)}, u32[]{:S(2)}) async-start(bf16[4,128,512]{2,1,0:T(8,128)(2,1)} %gather_fusion.2), calls=%async_computation.2 | async-start | bytes 1048576 | tf_op jit(solution)/shard_map/all_to_all | solution.py:66
  35.3 5.1 copy-start.10
  35.3 72.9 %all-to-all-start.1 = ((bf16[8,64,512]{2,1,0:T(8,128)(2,1)}), bf16[8,64,512]{2,1,0:T(8,128)(2,1)}, u32[]{:S(2)}, u32[]{:S(2)}) async-start(bf16[8,64,512]{2,1,0:T(8,128)(2,1)} %gather_fusion.1), calls=%async_computation.1 | async-start | bytes 1048576 | tf_op jit(solution)/shard_map/all_to_all | solution.py:69
  40.4 143.0 %all-reduce.13.cloned.1.call-start = ((), (), s32[]{:S(2)}) async-start(), calls=%async_computation.8 | async-start | bytes 1048576 | tf_op jit(solution)/shard_map/psum | solution.py:15
  105.2 1.7 copy-start.14
  106.2 126.7 %all-reduce.15.cloned.1.call-start = ((), (), s32[]{:S(2)}) async-start(), calls=%async_computation.9 | async-start | bytes 1048576 | tf_op jit(solution)/shard_map/psum | solution.py:15
  108.3 141.9 %all-to-all-start.3 = ((bf16[8,64,512]{2,1,0:T(8,128)(2,1)}), bf16[8,64,512]{2,1,0:T(8,128)(2,1)}, u32[]{:S(2)}, u32[]{:S(2)}) async-start(bf16[8,64,512]{2,1,0:T(8,128)(2,1)} %gather_fusion.3), calls=%async_computation.3 | async-start | bytes 1048576 | tf_op jit(solution)/shard_map/all_to_all | solution.py:69
  129.6 188.2 %all-reduce.17.cloned.1.call-start = ((), (), s32[]{:S(2)}) async-start(), calls=%async_computation.10 | async-start | bytes 1048576 | tf_op jit(solution)/shard_map/psum | solution.py:15
  247.1 1.7 copy-start.16
  247.1 7.3 %copy-start.13 = (s32[8]{0:T(128)S(1)}, s32[8]{0:T(128)}, u32[]{:S(2)}) copy-start(s32[8]{0:T(128)} %constant.219) | copy-start | bytes 100
  248.2 118.8 %all-reduce.19.cloned.1.call-start = ((), (), s32[]{:S(2)}) async-start(), calls=%async_computation.11 | async-start | bytes 1048576 | tf_op jit(solution)/shard_map/psum | solution.py:15
  250.2 123.5 %all-to-all-start.4 = ((bf16[4,128,512]{2,1,0:T(8,128)(2,1)}), bf16[4,128,512]{2,1,0:T(8,128)(2,1)}, u32[]{:S(2)}, u32[]{:S(2)}) async-start(bf16[4,128,512]{2,1,0:T(8,128)(2,1)} %gather_fusion.4), calls=%async_computation.4 | async-start | bytes 1048576 | tf_op jit(solution)/shard_map/all_to_all | solution.py:66
  373.7 40.0 %all-to-all-start.5 = ((bf16[8,64,512]{2,1,0:T(8,128)(2,1)}), bf16[8,64,512]{2,1,0:T(8,128)(2,1)S(1)}, u32[]{:S(2)}, u32[]{:S(2)}) async-start(bf16[8,64,512]{2,1,0:T(8,128)(2,1)} %gather_fusion.5), calls=%async_computation.5 | async-start | bytes 1048576 | tf_op jit(solution)/shard_map/all_to_all | solution.py:69
  400.1 59.0 %all-reduce.21.cloned.1.call-start = ((), (), s32[]{:S(2)}) async-start(), calls=%async_computation.12 | async-start | bytes 1048576 | tf_op jit(solution)/shard_map/psum | solution.py:15
  401.2 107.5 %all-reduce.23.cloned.1.call-start = ((), (), s32[]{:S(2)}) async-start(), calls=%async_computation.13 | async-start | bytes 1048576 | tf_op jit(solution)/shard_map/psum | solution.py:15
  508.8 0.8 copy-start.12
  513.0 1.0 copy-start.1
Sparse Core Ops, SparseCore 0:
  9.2 48.4 all-gather.2
  59.3 36.2 all-gather.4
  106.4 77.0 all-reduce.12
  186.6 46.2 all-reduce.14
  248.3 69.4 all-reduce.16
  320.7 46.2 all-reduce.18
  403.3 55.8 all-reduce.20
  462.4 46.2 all-reduce.22
where the time goes:
time: 531 us; the launch traced here: 521 us
  waiting for transfers between devices  394 us (74%)
  starting transfers between devices  64.6 us (12%)
  loops' own time  20.8 us (4%)
  between operations  14.2 us (3%)
  matrix products  13.1 us (2%)
  local copies, waits for them, and re-layouts  11.1 us (2%)
    psum x6, waiting for transfers between devices, from_root(): return lax.psum(jnp.where(mine, array, jnp.zeros_like(array)), axis)  310 us
    all_to_all x3, starting transfers between devices, per_device(): lax.all_to_all(b_tiles[b_rows, 0], 'row', split_axis=0, concat_axis=0, ti...  52.9 us
    all_gather x1, waiting for transfers between devices, per_device(): v_stack = lax.all_gather(v_powers, 'row', axis=2, tiled=True)[0]  37.9 us
    another operation x3, loops' own time, per_device(): current = lax.cond(my_front == front, solve, keep, current)  20.8 us
    all_gather x1, waiting for transfers between devices, per_device(): u_stack = lax.all_gather(u_powers, 'col', axis=2, tiled=True)[0]  17.1 us
    all_to_all x3, waiting for transfers between devices, per_device(): lax.all_to_all(a_tiles[0, a_rows], 'col', split_axis=0, concat_axis=0, ti...  14.9 us
    all_to_all x3, waiting for transfers between devices, per_device(): lax.all_to_all(b_tiles[b_rows, 0], 'row', split_axis=0, concat_axis=0, ti...  11.7 us
    all_to_all x3, starting transfers between devices, per_device(): lax.all_to_all(a_tiles[0, a_rows], 'col', split_axis=0, concat_axis=0, ti...  11.5 us
  transfers between devices with their start and end apart: 14, of which 11 were waited for; matrix products, arithmetic and copies ran while one was open for 4% of the time, Pallas kernels for 0%

commit v1 on v0

v1 whole, which is shorter than its diff:
```python
import functools
import jax
import jax.numpy as jnp
from jax import lax
from jax.experimental import pallas as pl
from jax.experimental.pallas import tpu as pltpu
from jax.sharding import PartitionSpec as P

FRONTS = 3
CHUNKS = 4
MESH = pl.DeviceIdType.MESH
BF = jnp.bfloat16
F32 = jnp.float32


def dot(left, right):
    return jnp.dot(left, right, preferred_element_type=F32)


def split(value):
    high = value.astype(BF)
    return high, (value - high.astype(F32)).astype(BF)


def product(left, right):
    (lh, ll), (rh, rl) = left, right
    return dot(lh, rh) + (dot(lh, rl) + dot(ll, rh))


def kernel(rows, cols, first, work, a, b, u, v, shift, out,
           s, ubuf, vbuf, uh, ul, vh, vl, yh, yl, xs, abuf, bbuf, xd, xa,
           loc, usend, urecv, vsend, vrecv, asend, arecv, aloc, bsend, brecv, bloc,
           dsend, xsend, fsend, xdrecv, xarecv):
    r = lax.axis_index("row")
    c = lax.axis_index("col")
    width = s.shape[0]
    half = width // 2
    hr = u.shape[2]
    hv = v.shape[2]
    ch = width // CHUNKS
    mine = r + c - first
    solver = (mine >= 0) & (mine < FRONTS)
    even = lax.rem(r, 2) == 0

    def remote(src, dst, ssem, rsem, to_row, to_col):
        return pltpu.make_async_remote_copy(
            src_ref=src, dst_ref=dst, send_sem=ssem, recv_sem=rsem,
            device_id=(to_row, to_col), device_id_type=MESH)

    def arrived(ref, sem):
        pltpu.make_async_copy(ref, ref, sem).wait()

    def span(count, body):
        def step(at, carry):
            body(at)
            return carry
        lax.fori_loop(0, count, step, 0)

    own_u = pl.ds(pl.multiple_of(c * hr, hr), hr)
    own_v = pl.ds(pl.multiple_of(r * hv, hv), hv)
    lo_half, hi_half = pl.ds(0, half), pl.ds(half, half)

    load_s = pltpu.make_async_copy(work, s, loc.at[0])
    load_u = pltpu.make_async_copy(u.at[0, 0], ubuf.at[own_u], loc.at[1])
    load_v = pltpu.make_async_copy(v.at[0, 0], vbuf.at[own_v], loc.at[2])
    load_s.start()

    @pl.when(solver)
    def _():
        load_u.start()
        load_v.start()

    barrier = pltpu.get_barrier_semaphore()

    def greet_row(at):
        @pl.when(at != r)
        def _():
            pl.semaphore_signal(barrier, inc=1, device_id=(at, c), device_id_type=MESH)

    def greet_col(at):
        @pl.when(at != c)
        def _():
            pl.semaphore_signal(barrier, inc=1, device_id=(r, at), device_id_type=MESH)

    span(rows, greet_row)
    span(cols, greet_col)
    pl.semaphore_wait(barrier, rows + cols - 2)

    def factors(act):
        def step(f):
            j = first + f - r

            @pl.when((j >= 0) & (j < cols) & (j != c))
            def _():
                act(remote(u.at[0, 0, :, lo_half], ubuf.at[own_u, lo_half],
                           usend.at[f, 0], urecv.at[c, 0], r, j))

                @pl.when(c * hr + hr > half)
                def _():
                    act(remote(u.at[0, 0, :, hi_half], ubuf.at[own_u, hi_half],
                               usend.at[f, 1], urecv.at[c, 1], r, j))

            i = first + f - c

            @pl.when((i >= 0) & (i < rows) & (i != r))
            def _():
                act(remote(v.at[0, 0, :, hi_half], vbuf.at[own_v, hi_half],
                           vsend.at[f, 1], vrecv.at[r, 1], i, c))

                @pl.when(r * hv < half)
                def _():
                    act(remote(v.at[0, 0, :, lo_half], vbuf.at[own_v, lo_half],
                               vsend.at[f, 0], vrecv.at[r, 0], i, c))
        span(FRONTS, step)

    def tiles(act, act_local):
        def step(f):
            def a_step(at):
                j = lax.rem(c + 1 + at, cols)
                k = first + f - j
                need = (r + j > first + f) & (k >= 0)

                @pl.when(need & (j != c))
                def _():
                    act(remote(a.at[0, k], abuf.at[f, own_u], asend.at[f, j], arecv.at[f, c], r, j))

                @pl.when(need & (j == c))
                def _():
                    act_local(pltpu.make_async_copy(a.at[0, k], abuf.at[f, own_u], aloc.at[f]))

            def b_step(l):
                i = first + f - l
                need = (i >= 0) & (i < rows) & (c > l)

                @pl.when(need & (i != r))
                def _():
                    act(remote(b.at[l, 0], bbuf.at[f, own_v], bsend.at[f, l], brecv.at[f, r], i, c))

                @pl.when(need & (i == r))
                def _():
                    act_local(pltpu.make_async_copy(b.at[l, 0], bbuf.at[f, own_v], bloc.at[f]))

            span(cols, a_step)
            span(cols, b_step)
        span(FRONTS, step)

    factors(lambda copy: copy.start())
    tiles(lambda copy: copy.start(), lambda copy: copy.start())
    load_s.wait()

    @pl.when(solver)
    def _():
        load_u.wait()
        load_v.wait()

        def u_wait(at):
            @pl.when(at != c)
            def _():
                place = pl.ds(pl.multiple_of(at * hr, hr), hr)
                arrived(ubuf.at[place, lo_half], urecv.at[at, 0])

                @pl.when(at * hr + hr > half)
                def _():
                    arrived(ubuf.at[place, hi_half], urecv.at[at, 1])

        def v_wait(at):
            @pl.when(at != r)
            def _():
                place = pl.ds(pl.multiple_of(at * hv, hv), hv)
                arrived(vbuf.at[place, hi_half], vrecv.at[at, 1])

                @pl.when(at * hv < half)
                def _():
                    arrived(vbuf.at[place, lo_half], vrecv.at[at, 0])

        span(cols, u_wait)
        span(rows, v_wait)

        def put(high, low, power, row_part, col_part, value):
            high[power, row_part, col_part], low[power, row_part, col_part] = split(value)

        t, e = slice(0, half), slice(half, width)
        for high, low, buf, corner in ((uh, ul, ubuf, (e, t)), (vh, vl, vbuf, (t, e))):
            for part in ((t, t), (e, e), corner):
                put(high, low, 0, *part, buf[part])
            for power in range(2):
                def get(part):
                    return high[(power,) + part], low[(power,) + part]
                for part in ((t, t), (e, e)):
                    put(high, low, power + 1, *part, product(get(part), get(part)))
                x, y = corner
                put(high, low, power + 1, x, y,
                    product(get((x, x)), get((x, y))) + product(get((x, y)), get((y, y))))

    def chunk(k):
        return pl.ds(pl.multiple_of(k * ch, ch), ch)

    def forwards(f, k, act):
        part = xd.at[f, chunk(k)]

        @pl.when(even)
        def _():
            act(remote(part, part, fsend.at[f, k, 0], xdrecv.at[f, k], r + 1, c))

            @pl.when(r + 2 < rows)
            def _():
                act(remote(part, part, fsend.at[f, k, 1], xdrecv.at[f, k], r + 2, c))

    def a_needed(f):
        return (mine > f) & (first + f - c >= 0)

    def b_needed(f):
        return (mine > f) & (first + f - r >= 0)

    def update(f):
        @pl.when(a_needed(f))
        def _():
            arrived(abuf.at[f, own_u], aloc.at[f])

            def a_wait(at):
                @pl.when(at != c)
                def _():
                    arrived(abuf.at[f, pl.ds(pl.multiple_of(at * hr, hr), hr)], arecv.at[f, at])

            def x_wait(k):
                arrived(xd.at[f, chunk(k)], xdrecv.at[f, k])
                forwards(f, k, lambda copy: copy.start())

            span(cols, a_wait)
            span(CHUNKS, x_wait)
            s[...] -= dot(abuf[f], xd[f])

        @pl.when(b_needed(f))
        def _():
            arrived(bbuf.at[f, own_v], bloc.at[f])

            def b_wait(at):
                @pl.when(at != r)
                def _():
                    arrived(bbuf.at[f, pl.ds(pl.multiple_of(at * hv, hv), hv)], brecv.at[f, at])

            span(rows, b_wait)
            span(CHUNKS, lambda k: arrived(xa.at[f, chunk(k)], xarecv.at[f, k]))
            s[...] -= dot(xa[f], bbuf[f])

    span(FRONTS, update)

    def spread(k, act):
        part = xs.at[chunk(k)]
        there, beside = xd.at[mine, chunk(k)], xa.at[mine, chunk(k)]

        @pl.when(r + 1 < rows)
        def _():
            act(remote(part, there, dsend.at[k, 0], xdrecv.at[mine, k], r + 1, c))

        def across(at):
            j = c + 1 + at

            @pl.when(j < cols)
            def _():
                act(remote(part, beside, xsend.at[k, at], xarecv.at[mine, k], r, j))

        span(cols - 1, across)

        @pl.when(even & (r + 2 < rows))
        def _():
            act(remote(part, there, dsend.at[k, 1], xdrecv.at[mine, k], r + 2, c))

    @pl.when(solver)
    def _():
        inverse = 0.5 / jnp.broadcast_to(shift[0], (1, width)).astype(F32)
        for part, extent in ((slice(0, half), half), (slice(half, width), width)):
            now = s[part, :]
            yh[0, part, :], yl[0, part, :] = split(now)
            for stage in range(FRONTS + 1):
                power = max(stage - 1, 0)
                moved = product((uh[power, part, :extent], ul[power, part, :extent]),
                                (yh[stage, :extent, :], yl[stage, :extent, :]))
                if stage == 0:
                    moved = now - moved
                mh, ml = split(moved)
                left = product((mh[:, :half], ml[:, :half]),
                               (vh[power, :half, :half], vl[power, :half, :half]))
                right = product((mh, ml), (vh[power, :, half:], vl[power, :, half:]))
                turned = jnp.concatenate([left, right], axis=1)
                now = (moved - turned) * inverse if stage == 0 else now + turned
                if stage < FRONTS:
                    yh[stage + 1, part, :], yl[stage + 1, part, :] = split(now)
            s[part, :] = now
            xs[part, :] = now.astype(BF)
            for k in range(CHUNKS):
                if part.start <= k * ch < part.stop:
                    spread(k, lambda copy: copy.start())

    store = pltpu.make_async_copy(s, out, loc.at[0])
    store.start()
    factors(lambda copy: copy.wait_send())
    tiles(lambda copy: copy.wait_send(), lambda copy: None)

    def drain(f):
        @pl.when(a_needed(f))
        def _():
            span(CHUNKS, lambda k: forwards(f, k, lambda copy: copy.wait_send()))

    span(FRONTS, drain)

    @pl.when(solver)
    def _():
        span(CHUNKS, lambda k: spread(k, lambda copy: copy.wait_send()))

    store.wait()


def per_device(rows, cols, work, a, b, u, v, shift):
    first = max(0, (rows + cols) // 2 - FRONTS)
    width = work.shape[0]
    tile = (width, width)
    any_ref = pl.BlockSpec(memory_space=pl.ANY)
    dma = pltpu.SemaphoreType.DMA
    stack = [pltpu.VMEM((FRONTS,) + tile, BF)]
    return pl.pallas_call(
        functools.partial(kernel, rows, cols, first),
        out_shape=jax.ShapeDtypeStruct(work.shape, work.dtype),
        in_specs=[any_ref] * 5 + [pl.BlockSpec(memory_space=pltpu.SMEM)],
        out_specs=any_ref,
        scratch_shapes=[pltpu.VMEM(tile, F32)] * 3 + stack * 4
        + [pltpu.VMEM((FRONTS + 1,) + tile, BF)] * 2
        + [pltpu.VMEM(tile, BF)] + stack * 4
        + [dma((3,)), dma((FRONTS, 2)), dma((cols, 2)), dma((FRONTS, 2)), dma((rows, 2)),
           dma((FRONTS, cols)), dma((FRONTS, cols)), dma((FRONTS,)),
           dma((FRONTS, cols)), dma((FRONTS, rows)), dma((FRONTS,)),
           dma((CHUNKS, 2)), dma((CHUNKS, cols - 1)), dma((FRONTS, CHUNKS, 2)),
           dma((FRONTS, CHUNKS)), dma((FRONTS, CHUNKS))],
        compiler_params=pltpu.CompilerParams(
            collective_id=0, has_side_effects=True, vmem_limit_bytes=48 * 1024 * 1024),
    )(work, a, b, u, v, shift)


def solution(mesh):
    placed = (
        P("row", "col"),
        P("row", None, "col", None),
        P(None, "col", "row", None),
        P("row", None, "col", None),
        P("col", None, "row", None),
        P(),
    )
    return jax.shard_map(
        functools.partial(per_device, mesh.shape["row"], mesh.shape["col"]),
        mesh=mesh, in_specs=placed, out_specs=P("row", "col"), check_vma=False
    )
```

time: 531 us -> 77.2 us (0.15)
  the two profiles are of different devices: /device:TPU:24 before, /device:TPU:31 now
where the time goes in v1:
time: 77.2 us; the launch traced here: 76.9 us
  Pallas kernels  69.7 us (90%)
  local copies, waits for them, and re-layouts  6.49 us (8%)
    pallas_call x1, Pallas kernels, per_device(): pl.pallas_call(functools.partial(kernel, rows, cols, first), out_shape=ja...  69.7 us
    unnamed x11, local copies, waits for them, and re-layouts  6.49 us

profile of v1, /device:TPU:31, one launch (start us, length us, event | category | flops | bytes accessed | tf_op | source)
XLA Modules:
  0.0 76.9 jit_solution(17919296679287678192)
XLA Ops:
  0.7 0.0 copy-start
  0.7 1.2 %copy-done = f32[512,512]{1,0:T(8,128)S(1)} copy-done((f32[512,512]{1,0:T(8,128)S(1)}, f32[512,512]{1,0:T(8,128)}, u32[]{:S(2)}) %copy-start) | copy-done | bytes 1048600
  1.9 0.0 copy-start.1
  1.9 1.2 %copy-done.1 = bf16[1,8,128,512]{3,2,1,0:T(8,128)(2,1)S(1)} copy-done((bf16[1,8,128,512]{3,2,1,0:T(8,128)(2,1)S(1)}, bf16[1,8,128,512]{3,2,1,0:T(8,128)(2,1)}, u32[]{:S(2)}) %copy-start.1) | copy-done | bytes 1048600
  3.1 0.0 copy-start.2
  3.1 1.1 %copy-done.2 = f32[1,3,128,512]{3,2,1,0:T(8,128)S(1)} copy-done((f32[1,3,128,512]{3,2,1,0:T(8,128)S(1)}, f32[1,3,128,512]{3,2,1,0:T(8,128)}, u32[]{:S(2)}) %copy-start.2) | copy-done | bytes 786456
  4.2 0.0 copy-start.3
  4.2 1.0 %copy-done.3 = f32[1,3,64,512]{3,2,1,0:T(8,128)S(1)} copy-done((f32[1,3,64,512]{3,2,1,0:T(8,128)S(1)}, f32[1,3,64,512]{3,2,1,0:T(8,128)}, u32[]{:S(2)}) %copy-start.3) | copy-done | bytes 393240
  5.2 0.0 copy-start.4
  5.2 0.9 %copy-done.4 = bf16[4,1,64,512]{3,2,1,0:T(8,128)(2,1)S(1)} copy-done((bf16[4,1,64,512]{3,2,1,0:T(8,128)(2,1)S(1)}, bf16[4,1,64,512]{3,2,1,0:T(8,128)(2,1)}, u32[]{:S(2)}) %copy-start.4) | copy-done | bytes 262168
  6.2 69.7 %shard_map.64 = f32[512,512]{1,0:T(8,128)S(1)} custom-call(f32[512,512]{1,0:T(8,128)S(1)} %copy-done, bf16[1,8,128,512]{3,2,1,0:T(8,128)(2,1)S(1)} %copy-done.1, bf16[4,1,64,512]{3,2,1,0:T(8,128)(2,1)S(1)} %copy-done.4, f32[1,3,128,512]{3,2,1,0:T(8,128)S(1)} %copy-done.2, f32[1,3,64,512]{3,2,1,0:T(8,128)S(1)} %copy-done.3, f32[1]{0:T(128)S(6)} %copy.8.shift), custom_call_target="tpu_custom_call" | custom-call | tf_op jit(solution)/shard_map/pallas_call | solution.py:321
  75.9 1.0 %copy.9 = f32[512,512]{1,0:T(8,128)} copy(f32[512,512]{1,0:T(8,128)S(1)} %shard_map.64) | data formatting | bytes 2097152
Async XLA Ops:
  0.7 1.2 %copy-start = (f32[512,512]{1,0:T(8,128)S(1)}, f32[512,512]{1,0:T(8,128)}, u32[]{:S(2)}) copy-start(f32[512,512]{1,0:T(8,128)} %work.1) | copy-start | bytes 3145732
  1.9 1.2 %copy-start.1 = (bf16[1,8,128,512]{3,2,1,0:T(8,128)(2,1)S(1)}, bf16[1,8,128,512]{3,2,1,0:T(8,128)(2,1)}, u32[]{:S(2)}) copy-start(bf16[1,8,128,512]{3,2,1,0:T(8,128)(2,1)} %a.1) | copy-start | bytes 3145732
  3.1 1.1 %copy-start.2 = (f32[1,3,128,512]{3,2,1,0:T(8,128)S(1)}, f32[1,3,128,512]{3,2,1,0:T(8,128)}, u32[]{:S(2)}) copy-start(f32[1,3,128,512]{3,2,1,0:T(8,128)} %u.1) | copy-start | bytes 2359300
  4.2 1.0 %copy-start.3 = (f32[1,3,64,512]{3,2,1,0:T(8,128)S(1)}, f32[1,3,64,512]{3,2,1,0:T(8,128)}, u32[]{:S(2)}) copy-start(f32[1,3,64,512]{3,2,1,0:T(8,128)} %v.1) | copy-start | bytes 1179652
  5.2 0.9 %copy-start.4 = (bf16[4,1,64,512]{3,2,1,0:T(8,128)(2,1)S(1)}, bf16[4,1,64,512]{3,2,1,0:T(8,128)(2,1)}, u32[]{:S(2)}) copy-start(bf16[4,1,64,512]{3,2,1,0:T(8,128)(2,1)} %b.1) | copy-start | bytes 786436

commit v2 on v1

--- a/solution.py
+++ b/solution.py
@@ -7,7 +7,8 @@
 from jax.sharding import PartitionSpec as P
 
 FRONTS = 3
-CHUNKS = 4
+CHUNKS = 8
+LANES = 128
 MESH = pl.DeviceIdType.MESH
 BF = jnp.bfloat16
 F32 = jnp.float32
@@ -41,6 +42,8 @@
     mine = r + c - first
     solver = (mine >= 0) & (mine < FRONTS)
     even = lax.rem(r, 2) == 0
+    last = mine == FRONTS - 1
+    blocks = width // LANES
 
     def remote(src, dst, ssem, rsem, to_row, to_col):
         return pltpu.make_async_remote_copy(
@@ -58,7 +61,6 @@
 
     own_u = pl.ds(pl.multiple_of(c * hr, hr), hr)
     own_v = pl.ds(pl.multiple_of(r * hv, hv), hv)
-    lo_half, hi_half = pl.ds(0, half), pl.ds(half, half)
 
     load_s = pltpu.make_async_copy(work, s, loc.at[0])
     load_u = pltpu.make_async_copy(u.at[0, 0], ubuf.at[own_u], loc.at[1])
@@ -67,6 +69,12 @@
 
     @pl.when(solver)
     def _():
+        for low in range(blocks):
+            for high in range(low + 1, blocks):
+                if low * LANES // half == high * LANES // half:
+                    x, y = pl.ds(low * LANES, LANES), pl.ds(high * LANES, LANES)
+                    ubuf[x, y] = jnp.zeros((LANES, LANES), F32)
+                    vbuf[y, x] = jnp.zeros((LANES, LANES), F32)
         load_u.start()
         load_v.start()
 
@@ -86,32 +94,34 @@
     span(cols, greet_col)
     pl.semaphore_wait(barrier, rows + cols - 2)
 
-    def factors(act):
-        def step(f):
-            j = first + f - r
-
-            @pl.when((j >= 0) & (j < cols) & (j != c))
-            def _():
-                act(remote(u.at[0, 0, :, lo_half], ubuf.at[own_u, lo_half],
-                           usend.at[f, 0], urecv.at[c, 0], r, j))
-
-                @pl.when(c * hr + hr > half)
-                def _():
-                    act(remote(u.at[0, 0, :, hi_half], ubuf.at[own_u, hi_half],
-                               usend.at[f, 1], urecv.at[c, 1], r, j))
-
-            i = first + f - c
-
-            @pl.when((i >= 0) & (i < rows) & (i != r))
-            def _():
-                act(remote(v.at[0, 0, :, hi_half], vbuf.at[own_v, hi_half],
-                           vsend.at[f, 1], vrecv.at[r, 1], i, c))
-
-                @pl.when(r * hv < half)
-                def _():
-                    act(remote(v.at[0, 0, :, lo_half], vbuf.at[own_v, lo_half],
-                               vsend.at[f, 0], vrecv.at[r, 0], i, c))
-        span(FRONTS, step)
+    def u_filled(at, body):
+        reach = (at * hr + hr - 1) // LANES
+        for block in range(blocks):
+            @pl.when(reach == block)
+            def _():
+                body(pl.ds(0, (block + 1) * LANES))
+
+    def v_filled(at, body):
+        reach = at * hv // LANES
+        for block in range(blocks):
+            @pl.when(reach == block)
+            def _():
+                body(pl.ds(block * LANES, width - block * LANES))
+
+    def factors(f, act):
+        j = first + f - r
+
+        @pl.when((j >= 0) & (j < cols) & (j != c))
+        def _():
+            u_filled(c, lambda part: act(remote(
+                u.at[0, 0, :, part], ubuf.at[own_u, part], usend.at[f], urecv.at[c], r, j)))
+
+        i = first + f - c
+
+        @pl.when((i >= 0) & (i < rows) & (i != r))
+        def _():
+            v_filled(r, lambda part: act(remote(
+                v.at[0, 0, :, part], vbuf.at[own_v, part], vsend.at[f], vrecv.at[r], i, c)))
 
     def tiles(act, act_local):
         def step(f):
@@ -144,53 +154,73 @@
             span(cols, b_step)
         span(FRONTS, step)
 
-    factors(lambda copy: copy.start())
-    tiles(lambda copy: copy.start(), lambda copy: copy.start())
+    factors(0, lambda copy: copy.start())
     load_s.wait()
+    factors(0, lambda copy: copy.wait_send())
+    for f in range(1, FRONTS):
+        factors(f, lambda copy: copy.start())
+
+    t, e = slice(0, half), slice(half, width)
+
+    def prepare(high, low, buf, corner, scale):
+        x, y = corner
+
+        def put(slot, part, value):
+            high[(slot,) + part], low[(slot,) + part] = split(value)
+
+        def get(slot, part):
+            return high[(slot,) + part], low[(slot,) + part]
+
+        def square(slot, part):
+            if part != corner:
+                return product(get(slot, part), get(slot, part))
+            return (product(get(slot, (x, x)), get(slot, corner))
+                    + product(get(slot, corner), get(slot, (y, y))))
+
+        parts = ((t, t), (e, e), corner)
+        eye = (lax.broadcasted_iota(jnp.int32, (half, half), 0)
+               == lax.broadcasted_iota(jnp.int32, (half, half), 1)).astype(F32)
+        for part in parts:
+            put(4, part, buf[part])
+        for part in parts:
+            base = buf[part]
+            put(0, part, ((eye - base) if part != corner else -base) * scale)
+        for part in parts:
+            value = square(4, part)
+            put(2, part, value)
+            put(1, part, (buf[part] - value) * scale)
+        for part in parts:
+            put(3, part, square(2, part))
 
     @pl.when(solver)
     def _():
         load_u.wait()
-        load_v.wait()
 
         def u_wait(at):
             @pl.when(at != c)
             def _():
                 place = pl.ds(pl.multiple_of(at * hr, hr), hr)
-                arrived(ubuf.at[place, lo_half], urecv.at[at, 0])
-
-                @pl.when(at * hr + hr > half)
-                def _():
-                    arrived(ubuf.at[place, hi_half], urecv.at[at, 1])
+                u_filled(at, lambda part: arrived(ubuf.at[place, part], urecv.at[at]))
+
+        span(cols, u_wait)
+        prepare(uh, ul, ubuf, (e, t), 1.0)
+
+    for f in range(1, FRONTS):
+        factors(f, lambda copy: copy.wait_send())
+    tiles(lambda copy: copy.start(), lambda copy: copy.start())
+
+    @pl.when(solver)
+    def _():
+        load_v.wait()
 
         def v_wait(at):
             @pl.when(at != r)
             def _():
                 place = pl.ds(pl.multiple_of(at * hv, hv), hv)
-                arrived(vbuf.at[place, hi_half], vrecv.at[at, 1])
-
-                @pl.when(at * hv < half)
-                def _():
-                    arrived(vbuf.at[place, lo_half], vrecv.at[at, 0])
-
-        span(cols, u_wait)
+                v_filled(at, lambda part: arrived(vbuf.at[place, part], vrecv.at[at]))
+
         span(rows, v_wait)
-
-        def put(high, low, power, row_part, col_part, value):
-            high[power, row_part, col_part], low[power, row_part, col_part] = split(value)
-
-        t, e = slice(0, half), slice(half, width)
-        for high, low, buf, corner in ((uh, ul, ubuf, (e, t)), (vh, vl, vbuf, (t, e))):
-            for part in ((t, t), (e, e), corner):
-                put(high, low, 0, *part, buf[part])
-            for power in range(2):
-                def get(part):
-                    return high[(power,) + part], low[(power,) + part]
-                for part in ((t, t), (e, e)):
-                    put(high, low, power + 1, *part, product(get(part), get(part)))
-                x, y = corner
-                put(high, low, power + 1, x, y,
-                    product(get((x, x)), get((x, y))) + product(get((x, y)), get((y, y))))
+        prepare(vh, vl, vbuf, (t, e), 0.5 / jnp.broadcast_to(shift[0], (1, half)).astype(F32))
 
     def chunk(k):
         return pl.ds(pl.multiple_of(k * ch, ch), ch)
@@ -245,56 +275,80 @@
 
     span(FRONTS, update)
 
-    def spread(k, act):
+    def urgent(k, act):
         part = xs.at[chunk(k)]
-        there, beside = xd.at[mine, chunk(k)], xa.at[mine, chunk(k)]
 
         @pl.when(r + 1 < rows)
         def _():
-            act(remote(part, there, dsend.at[k, 0], xdrecv.at[mine, k], r + 1, c))
+            act(remote(part, xd.at[mine, chunk(k)], dsend.at[k, 0], xdrecv.at[mine, k], r + 1, c))
+
+        @pl.when(c + 1 < cols)
+        def _():
+            act(remote(part, xa.at[mine, chunk(k)], xsend.at[k, 0], xarecv.at[mine, k], r, c + 1))
+
+    def others(k, act):
+        part = xs.at[chunk(k)]
+
+        @pl.when(even & (r + 2 < rows))
+        def _():
+            act(remote(part, xd.at[mine, chunk(k)], dsend.at[k, 1], xdrecv.at[mine, k], r + 2, c))
 
         def across(at):
-            j = c + 1 + at
-
-            @pl.when(j < cols)
-            def _():
-                act(remote(part, beside, xsend.at[k, at], xarecv.at[mine, k], r, j))
-
-        span(cols - 1, across)
-
-        @pl.when(even & (r + 2 < rows))
-        def _():
-            act(remote(part, there, dsend.at[k, 1], xdrecv.at[mine, k], r + 2, c))
+            @pl.when(c + at < cols)
+            def _():
+                act(remote(part, xa.at[mine, chunk(k)], xsend.at[k, at - 1],
+                           xarecv.at[mine, k], r, c + at))
+
+        span(cols - 2, lambda at: across(at + 2))
+
+    def start(copy):
+        copy.start()
+
+    def sent(copy):
+        copy.wait_send()
 
     @pl.when(solver)
     def _():
-        inverse = 0.5 / jnp.broadcast_to(shift[0], (1, width)).astype(F32)
-        for part, extent in ((slice(0, half), half), (slice(half, width), width)):
+        for part, extent in ((t, half), (e, width)):
             now = s[part, :]
             yh[0, part, :], yl[0, part, :] = split(now)
-            for stage in range(FRONTS + 1):
-                power = max(stage - 1, 0)
-                moved = product((uh[power, part, :extent], ul[power, part, :extent]),
-                                (yh[stage, :extent, :], yl[stage, :extent, :]))
-                if stage == 0:
-                    moved = now - moved
-                mh, ml = split(moved)
-                left = product((mh[:, :half], ml[:, :half]),
-                               (vh[power, :half, :half], vl[power, :half, :half]))
-                right = product((mh, ml), (vh[power, :, half:], vl[power, :, half:]))
-                turned = jnp.concatenate([left, right], axis=1)
-                now = (moved - turned) * inverse if stage == 0 else now + turned
-                if stage < FRONTS:
-                    yh[stage + 1, part, :], yl[stage + 1, part, :] = split(now)
+
+            def left(slot, stage):
+                return split(product((uh[slot, part, :extent], ul[slot, part, :extent]),
+                                     (yh[stage, :extent, :], yl[stage, :extent, :])))
+
+            def right(slot, moved):
+                high, low = moved
+                near = product((high[:, :half], low[:, :half]),
+                               (vh[slot, :half, :half], vl[slot, :half, :half]))
+                far = product((high, low), (vh[slot, :, half:], vl[slot, :, half:]))
+                return jnp.concatenate([near, far], axis=1)
+
+            zero, one = left(0, 0), left(1, 0)
+            now = right(0, zero) + right(1, one)
+            for stage in (1, 2):
+                yh[stage, part, :], yl[stage, part, :] = split(now)
+                now = now + right(stage + 1, left(stage + 1, stage))
             s[part, :] = now
             xs[part, :] = now.astype(BF)
-            for k in range(CHUNKS):
-                if part.start <= k * ch < part.stop:
-                    spread(k, lambda copy: copy.start())
+            lowest = part.start // ch
+
+            def send(at):
+                urgent(lowest + at, start)
+
+                @pl.when(last)
+                def _():
+                    others(lowest + at, start)
+
+            span(CHUNKS // 2, send)
+
+        @pl.when(jnp.logical_not(last))
+        def _():
+            span(CHUNKS, lambda k: urgent(k, sent))
+            span(CHUNKS, lambda k: others(k, start))
 
     store = pltpu.make_async_copy(s, out, loc.at[0])
     store.start()
-    factors(lambda copy: copy.wait_send())
     tiles(lambda copy: copy.wait_send(), lambda copy: None)
 
     def drain(f):
@@ -306,7 +360,11 @@
 
     @pl.when(solver)
     def _():
-        span(CHUNKS, lambda k: spread(k, lambda copy: copy.wait_send()))
+        span(CHUNKS, lambda k: others(k, sent))
+
+        @pl.when(last)
+        def _():
+            span(CHUNKS, lambda k: urgent(k, sent))
 
     store.wait()
 
@@ -323,16 +381,16 @@
         out_shape=jax.ShapeDtypeStruct(work.shape, work.dtype),
         in_specs=[any_ref] * 5 + [pl.BlockSpec(memory_space=pltpu.SMEM)],
         out_specs=any_ref,
-        scratch_shapes=[pltpu.VMEM(tile, F32)] * 3 + stack * 4
-        + [pltpu.VMEM((FRONTS + 1,) + tile, BF)] * 2
+        scratch_shapes=[pltpu.VMEM(tile, F32)] * 3 + [pltpu.VMEM((5,) + tile, BF)] * 4
+        + [pltpu.VMEM((3,) + tile, BF)] * 2
         + [pltpu.VMEM(tile, BF)] + stack * 4
-        + [dma((3,)), dma((FRONTS, 2)), dma((cols, 2)), dma((FRONTS, 2)), dma((rows, 2)),
+        + [dma((3,)), dma((FRONTS,)), dma((cols,)), dma((FRONTS,)), dma((rows,)),
            dma((FRONTS, cols)), dma((FRONTS, cols)), dma((FRONTS,)),
            dma((FRONTS, cols)), dma((FRONTS, rows)), dma((FRONTS,)),
            dma((CHUNKS, 2)), dma((CHUNKS, cols - 1)), dma((FRONTS, CHUNKS, 2)),
            dma((FRONTS, CHUNKS)), dma((FRONTS, CHUNKS))],
         compiler_params=pltpu.CompilerParams(
-            collective_id=0, has_side_effects=True, vmem_limit_bytes=48 * 1024 * 1024),
+            collective_id=0, has_side_effects=True, vmem_limit_bytes=63 * 1024 * 1024),
     )(work, a, b, u, v, shift)
 
 

time: 77.2 us -> 72.9 us (0.944)
  the two profiles are of different devices: /device:TPU:31 before, /device:TPU:29 now
where the time goes in v2:
time: 72.9 us; the launch traced here: 72.7 us
  Pallas kernels  69.8 us (96%)
  local copies, waits for them, and re-layouts  2.26 us (3%)
    pallas_call x1, Pallas kernels, per_device(): pl.pallas_call(functools.partial(kernel, rows, cols, first), out_shape=ja...  69.8 us
    unnamed x1, local copies, waits for them, and re-layouts  2.26 us

profile of v2, /device:TPU:29, one launch (start us, length us, event | category | flops | bytes accessed | tf_op | source)
XLA Modules:
  0.0 72.7 jit_solution(9733256286992480098)
XLA Ops:
  0.7 69.8 %shard_map.64 = f32[512,512]{1,0:T(8,128)} custom-call(f32[512,512]{1,0:T(8,128)} %work.1, bf16[1,8,128,512]{3,2,1,0:T(8,128)(2,1)} %a.1, bf16[4,1,64,512]{3,2,1,0:T(8,128)(2,1)} %b.1, f32[1,3,128,512]{3,2,1,0:T(8,128)} %u.1, f32[1,3,64,512]{3,2,1,0:T(8,128)} %v.1, f32[1]{0:T(128)S(6)} %copy.8.shift), custom_call_target="tpu_custom_call" | custom-call | tf_op jit(solution)/shard_map/pallas_call | solution.py:379
  70.5 2.3 %copy.9 = f32[512,512]{1,0:T(8,128)} copy(f32[512,512]{1,0:T(8,128)} %shard_map.64) | data formatting | bytes 2097152

commit v3 on v2

--- a/solution.py
+++ b/solution.py
@@ -31,7 +31,7 @@
 def kernel(rows, cols, first, work, a, b, u, v, shift, out,
            s, ubuf, vbuf, uh, ul, vh, vl, yh, yl, xs, abuf, bbuf, xd, xa,
            loc, usend, urecv, vsend, vrecv, asend, arecv, aloc, bsend, brecv, bloc,
-           dsend, xsend, fsend, xdrecv, xarecv):
+           dsend, xsend, fsend, ssend, xdrecv, xarecv, vpass, vgot):
     r = lax.axis_index("row")
     c = lax.axis_index("col")
     width = s.shape[0]
@@ -76,6 +76,9 @@
                     ubuf[x, y] = jnp.zeros((LANES, LANES), F32)
                     vbuf[y, x] = jnp.zeros((LANES, LANES), F32)
         load_u.start()
+
+    @pl.when(solver & (mine != 1))
+    def _():
         load_v.start()
 
     barrier = pltpu.get_barrier_semaphore()
@@ -118,47 +121,69 @@
 
         i = first + f - c
 
-        @pl.when((i >= 0) & (i < rows) & (i != r))
+        @pl.when((f != 1) & (i >= 0) & (i < rows) & (i != r))
         def _():
             v_filled(r, lambda part: act(remote(
                 v.at[0, 0, :, part], vbuf.at[own_v, part], vsend.at[f], vrecv.at[r], i, c)))
 
-    def tiles(act, act_local):
-        def step(f):
-            def a_step(at):
-                j = lax.rem(c + 1 + at, cols)
-                k = first + f - j
-                need = (r + j > first + f) & (k >= 0)
-
-                @pl.when(need & (j != c))
-                def _():
-                    act(remote(a.at[0, k], abuf.at[f, own_u], asend.at[f, j], arecv.at[f, c], r, j))
-
-                @pl.when(need & (j == c))
-                def _():
-                    act_local(pltpu.make_async_copy(a.at[0, k], abuf.at[f, own_u], aloc.at[f]))
-
-            def b_step(l):
-                i = first + f - l
-                need = (i >= 0) & (i < rows) & (c > l)
-
-                @pl.when(need & (i != r))
-                def _():
-                    act(remote(b.at[l, 0], bbuf.at[f, own_v], bsend.at[f, l], brecv.at[f, r], i, c))
-
-                @pl.when(need & (i == r))
-                def _():
-                    act_local(pltpu.make_async_copy(b.at[l, 0], bbuf.at[f, own_v], bloc.at[f]))
-
-            span(cols, a_step)
-            span(cols, b_step)
-        span(FRONTS, step)
-
-    factors(0, lambda copy: copy.start())
+    def tiles(f, near, act, act_local):
+        def a_step(at):
+            j = lax.rem(c + 1 + at, cols)
+            k = first + f - j
+            need = (r + j > first + f) & (k >= 0) & ((r + j == first + f + 1) == near)
+
+            @pl.when(need & (j != c))
+            def _():
+                act(remote(a.at[0, k], abuf.at[f, own_u], asend.at[f, j], arecv.at[f, c], r, j))
+
+            @pl.when(need & (j == c))
+            def _():
+                act_local(pltpu.make_async_copy(a.at[0, k], abuf.at[f, own_u], aloc.at[f]))
+
+        def b_step(l):
+            i = first + f - l
+            need = (i >= 0) & (i < rows) & (c > l) & ((c == l + 1) == near)
+
+            @pl.when(need & (i != r))
+            def _():
+                act(remote(b.at[l, 0], bbuf.at[f, own_v], bsend.at[f, l], brecv.at[f, r], i, c))
+
+            @pl.when(need & (i == r))
+            def _():
+                act_local(pltpu.make_async_copy(b.at[l, 0], bbuf.at[f, own_v], bloc.at[f]))
+
+        span(cols, a_step)
+        span(cols, b_step)
+
+    def start(copy):
+        copy.start()
+
+    def sent(copy):
+        copy.wait_send()
+
+    def nothing(copy):
+        return None
+
+    factors(0, start)
     load_s.wait()
-    factors(0, lambda copy: copy.wait_send())
-    for f in range(1, FRONTS):
-        factors(f, lambda copy: copy.start())
+
+    def send_ahead(paced):
+        for f in range(1, FRONTS):
+            if paced:
+                factors(f - 1, sent)
+                if f > 1:
+                    tiles(f - 2, True, sent, nothing)
+            factors(f, start)
+            tiles(f - 1, True, start, start)
+        if paced:
+            factors(FRONTS - 1, sent)
+            tiles(FRONTS - 2, True, sent, nothing)
+        tiles(FRONTS - 1, True, start, start)
+        span(FRONTS, lambda f: tiles(f, False, start, start))
+
+    @pl.when(mine != 0)
+    def _():
+        send_ahead(True)
 
     t, e = slice(0, half), slice(half, width)
 
@@ -205,11 +230,23 @@
         span(cols, u_wait)
         prepare(uh, ul, ubuf, (e, t), 1.0)
 
-    for f in range(1, FRONTS):
-        factors(f, lambda copy: copy.wait_send())
-    tiles(lambda copy: copy.start(), lambda copy: copy.start())
-
-    @pl.when(solver)
+    @pl.when(mine == 0)
+    def _():
+        send_ahead(False)
+
+    beside = jnp.where(even, r + 1, r - 1)
+    passing = solver & (mine != 1) & ((mine == 0) == even)
+
+    def pass_v(act):
+        for at, (x, y) in enumerate(((t, t), (slice(0, width), e))):
+            part = vbuf.at[pl.ds(x.start, x.stop - x.start), pl.ds(y.start, y.stop - y.start)]
+            act(remote(part, part, vpass.at[at], vgot.at[at], beside, c))
+
+    @pl.when(mine == 1)
+    def _():
+        pass_v(lambda copy: copy.wait_recv())
+
+    @pl.when(solver & (mine != 1))
     def _():
         load_v.wait()
 
@@ -220,6 +257,13 @@
                 v_filled(at, lambda part: arrived(vbuf.at[place, part], vrecv.at[at]))
 
         span(rows, v_wait)
+
+        @pl.when(passing)
+        def _():
+            pass_v(start)
+
+    @pl.when(solver)
+    def _():
         prepare(vh, vl, vbuf, (t, e), 0.5 / jnp.broadcast_to(shift[0], (1, half)).astype(F32))
 
     def chunk(k):
@@ -235,6 +279,17 @@
             @pl.when(r + 2 < rows)
             def _():
                 act(remote(part, part, fsend.at[f, k, 1], xdrecv.at[f, k], r + 2, c))
+
+    square = cols == 4
+
+    def sideways(f, k, act):
+        if square:
+            part = xa.at[f, chunk(k)]
+            source = first + f - r
+
+            @pl.when(((source == 0) & (c == 2)) | ((source == 1) & (c == 3) & (f == FRONTS - 1)))
+            def _():
+                act(remote(part, part, ssend.at[f, k], xarecv.at[f, k], r, 5 - c))
 
     def a_needed(f):
         return (mine > f) & (first + f - c >= 0)
@@ -270,42 +325,36 @@
                     arrived(bbuf.at[f, pl.ds(pl.multiple_of(at * hv, hv), hv)], brecv.at[f, at])
 
             span(rows, b_wait)
-            span(CHUNKS, lambda k: arrived(xa.at[f, chunk(k)], xarecv.at[f, k]))
+
+            def x_wait(k):
+                arrived(xa.at[f, chunk(k)], xarecv.at[f, k])
+                sideways(f, k, start)
+
+            span(CHUNKS, x_wait)
             s[...] -= dot(xa[f], bbuf[f])
 
     span(FRONTS, update)
 
-    def urgent(k, act):
+    def spread(k, act):
         part = xs.at[chunk(k)]
+        there, across = xd.at[mine, chunk(k)], xa.at[mine, chunk(k)]
 
         @pl.when(r + 1 < rows)
         def _():
-            act(remote(part, xd.at[mine, chunk(k)], dsend.at[k, 0], xdrecv.at[mine, k], r + 1, c))
-
-        @pl.when(c + 1 < cols)
-        def _():
-            act(remote(part, xa.at[mine, chunk(k)], xsend.at[k, 0], xarecv.at[mine, k], r, c + 1))
-
-    def others(k, act):
-        part = xs.at[chunk(k)]
+            act(remote(part, there, dsend.at[k, 0], xdrecv.at[mine, k], r + 1, c))
+
+        def right(at):
+            relayed = (c == 0) & (at == 3) | (c == 1) & (at == 1) & last if square else at < 0
+
+            @pl.when((c + at < cols) & jnp.logical_not(relayed))
+            def _():
+                act(remote(part, across, xsend.at[k, at - 1], xarecv.at[mine, k], r, c + at))
+
+        span(cols - 1, lambda at: right(at + 1))
 
         @pl.when(even & (r + 2 < rows))
         def _():
-            act(remote(part, xd.at[mine, chunk(k)], dsend.at[k, 1], xdrecv.at[mine, k], r + 2, c))
-
-        def across(at):
-            @pl.when(c + at < cols)
-            def _():
-                act(remote(part, xa.at[mine, chunk(k)], xsend.at[k, at - 1],
-                           xarecv.at[mine, k], r, c + at))
-
-        span(cols - 2, lambda at: across(at + 2))
-
-    def start(copy):
-        copy.start()
-
-    def sent(copy):
-        copy.wait_send()
+            act(remote(part, there, dsend.at[k, 1], xdrecv.at[mine, k], r + 2, c))
 
     @pl.when(solver)
     def _():
@@ -333,38 +382,39 @@
             xs[part, :] = now.astype(BF)
             lowest = part.start // ch
 
-            def send(at):
-                urgent(lowest + at, start)
-
-                @pl.when(last)
-                def _():
-                    others(lowest + at, start)
-
-            span(CHUNKS // 2, send)
-
-        @pl.when(jnp.logical_not(last))
-        def _():
-            span(CHUNKS, lambda k: urgent(k, sent))
-            span(CHUNKS, lambda k: others(k, start))
+            span(CHUNKS // 2, lambda at: spread(lowest + at, start))
 
     store = pltpu.make_async_copy(s, out, loc.at[0])
     store.start()
-    tiles(lambda copy: copy.wait_send(), lambda copy: None)
+
+    @pl.when(mine == 0)
+    def _():
+        for f in range(FRONTS):
+            factors(f, sent)
+        for f in range(FRONTS - 1):
+            tiles(f, True, sent, nothing)
+
+    tiles(FRONTS - 1, True, sent, nothing)
+    span(FRONTS, lambda f: tiles(f, False, sent, nothing))
 
     def drain(f):
         @pl.when(a_needed(f))
         def _():
-            span(CHUNKS, lambda k: forwards(f, k, lambda copy: copy.wait_send()))
+            span(CHUNKS, lambda k: forwards(f, k, sent))
+
+        @pl.when(b_needed(f))
+        def _():
+            span(CHUNKS, lambda k: sideways(f, k, sent))
 
     span(FRONTS, drain)
 
+    @pl.when(passing)
+    def _():
+        pass_v(sent)
+
     @pl.when(solver)
     def _():
-        span(CHUNKS, lambda k: others(k, sent))
-
-        @pl.when(last)
-        def _():
-            span(CHUNKS, lambda k: urgent(k, sent))
+        span(CHUNKS, lambda k: spread(k, sent))
 
     store.wait()
 
@@ -388,7 +438,7 @@
            dma((FRONTS, cols)), dma((FRONTS, cols)), dma((FRONTS,)),
            dma((FRONTS, cols)), dma((FRONTS, rows)), dma((FRONTS,)),
            dma((CHUNKS, 2)), dma((CHUNKS, cols - 1)), dma((FRONTS, CHUNKS, 2)),
-           dma((FRONTS, CHUNKS)), dma((FRONTS, CHUNKS))],
+           dma((FRONTS, CHUNKS)), dma((FRONTS, CHUNKS)), dma((FRONTS, CHUNKS)), dma((2,)), dma((2,))],
         compiler_params=pltpu.CompilerParams(
             collective_id=0, has_side_effects=True, vmem_limit_bytes=63 * 1024 * 1024),
     )(work, a, b, u, v, shift)

time: 72.9 us -> 72.5 us (level)
  the two profiles are of different devices: /device:TPU:29 before, /device:TPU:20 now
where the time goes in v3:
time: 72.5 us; the launch traced here: 72.3 us
  Pallas kernels  69.4 us (96%)
  local copies, waits for them, and re-layouts  2.26 us (3%)
    pallas_call x1, Pallas kernels, per_device(): pl.pallas_call(functools.partial(kernel, rows, cols, first), out_shape=ja...  69.4 us
    unnamed x1, local copies, waits for them, and re-layouts  2.26 us

profile of v3, /device:TPU:20, one launch (start us, length us, event | category | flops | bytes accessed | tf_op | source)
XLA Modules:
  0.0 72.3 jit_solution(2691519657846582989)
XLA Ops:
  0.7 69.4 %shard_map.64 = f32[512,512]{1,0:T(8,128)} custom-call(f32[512,512]{1,0:T(8,128)} %work.1, bf16[1,8,128,512]{3,2,1,0:T(8,128)(2,1)} %a.1, bf16[4,1,64,512]{3,2,1,0:T(8,128)(2,1)} %b.1, f32[1,3,128,512]{3,2,1,0:T(8,128)} %u.1, f32[1,3,64,512]{3,2,1,0:T(8,128)} %v.1, f32[1]{0:T(128)S(6)} %copy.8.shift), custom_call_target="tpu_custom_call" | custom-call | tf_op jit(solution)/shard_map/pallas_call | solution.py:429
  70.1 2.3 %copy.9 = f32[512,512]{1,0:T(8,128)} copy(f32[512,512]{1,0:T(8,128)} %shard_map.64) | data formatting | bytes 2097152

commit v4 on v3

--- a/solution.py
+++ b/solution.py
@@ -28,8 +28,8 @@
     return dot(lh, rh) + (dot(lh, rl) + dot(ll, rh))
 
 
-def kernel(rows, cols, first, work, a, b, u, v, shift, out,
-           s, ubuf, vbuf, uh, ul, vh, vl, yh, yl, xs, abuf, bbuf, xd, xa,
+def kernel(rows, cols, first, work, a, b, u, v, shift, s,
+           ubuf, vbuf, uh, ul, vh, vl, yh, yl, xs, abuf, bbuf, xd, xa,
            loc, usend, urecv, vsend, vrecv, asend, arecv, aloc, bsend, brecv, bloc,
            dsend, xsend, fsend, ssend, xdrecv, xarecv, vpass, vgot):
     r = lax.axis_index("row")
@@ -126,31 +126,41 @@
             v_filled(r, lambda part: act(remote(
                 v.at[0, 0, :, part], vbuf.at[own_v, part], vsend.at[f], vrecv.at[r], i, c)))
 
-    def tiles(f, near, act, act_local):
+    def a_send(f, j, need, act, act_local):
+        k = first + f - j
+
+        @pl.when(need & (j != c))
+        def _():
+            act(remote(a.at[0, k], abuf.at[f, own_u], asend.at[f, j], arecv.at[f, c], r, j))
+
+        @pl.when(need & (j == c))
+        def _():
+            act_local(pltpu.make_async_copy(a.at[0, k], abuf.at[f, own_u], aloc.at[f]))
+
+    def b_send(f, l, need, act, act_local):
+        i = first + f - l
+
+        @pl.when(need & (i != r))
+        def _():
+            act(remote(b.at[l, 0], bbuf.at[f, own_v], bsend.at[f, l], brecv.at[f, r], i, c))
+
+        @pl.when(need & (i == r))
+        def _():
+            act_local(pltpu.make_async_copy(b.at[l, 0], bbuf.at[f, own_v], bloc.at[f]))
+
+    def near(f, act, act_local):
+        j, i = first + f + 1 - r, first + f + 1 - c
+        a_send(f, j, (j >= 0) & (j < cols) & (r >= 1), act, act_local)
+        b_send(f, c - 1, (i >= 0) & (i < rows) & (c >= 1), act, act_local)
+
+    def rest(f, act, act_local):
         def a_step(at):
             j = lax.rem(c + 1 + at, cols)
-            k = first + f - j
-            need = (r + j > first + f) & (k >= 0) & ((r + j == first + f + 1) == near)
-
-            @pl.when(need & (j != c))
-            def _():
-                act(remote(a.at[0, k], abuf.at[f, own_u], asend.at[f, j], arecv.at[f, c], r, j))
-
-            @pl.when(need & (j == c))
-            def _():
-                act_local(pltpu.make_async_copy(a.at[0, k], abuf.at[f, own_u], aloc.at[f]))
+            a_send(f, j, (r + j > first + f + 1) & (first + f - j >= 0), act, act_local)
 
         def b_step(l):
             i = first + f - l
-            need = (i >= 0) & (i < rows) & (c > l) & ((c == l + 1) == near)
-
-            @pl.when(need & (i != r))
-            def _():
-                act(remote(b.at[l, 0], bbuf.at[f, own_v], bsend.at[f, l], brecv.at[f, r], i, c))
-
-            @pl.when(need & (i == r))
-            def _():
-                act_local(pltpu.make_async_copy(b.at[l, 0], bbuf.at[f, own_v], bloc.at[f]))
+            b_send(f, l, (i >= 0) & (i < rows) & (c > l + 1), act, act_local)
 
         span(cols, a_step)
         span(cols, b_step)
@@ -172,18 +182,18 @@
             if paced:
                 factors(f - 1, sent)
                 if f > 1:
-                    tiles(f - 2, True, sent, nothing)
+                    near(f - 2, sent, nothing)
             factors(f, start)
-            tiles(f - 1, True, start, start)
+            near(f - 1, start, start)
         if paced:
             factors(FRONTS - 1, sent)
-            tiles(FRONTS - 2, True, sent, nothing)
-        tiles(FRONTS - 1, True, start, start)
-        span(FRONTS, lambda f: tiles(f, False, start, start))
+            near(FRONTS - 2, sent, nothing)
+        near(FRONTS - 1, start, start)
 
     @pl.when(mine != 0)
     def _():
         send_ahead(True)
+        span(FRONTS, lambda f: rest(f, start, start))
 
     t, e = slice(0, half), slice(half, width)
 
@@ -307,13 +317,7 @@
                 def _():
                     arrived(abuf.at[f, pl.ds(pl.multiple_of(at * hr, hr), hr)], arecv.at[f, at])
 
-            def x_wait(k):
-                arrived(xd.at[f, chunk(k)], xdrecv.at[f, k])
-                forwards(f, k, lambda copy: copy.start())
-
             span(cols, a_wait)
-            span(CHUNKS, x_wait)
-            s[...] -= dot(abuf[f], xd[f])
 
         @pl.when(b_needed(f))
         def _():
@@ -326,11 +330,25 @@
 
             span(rows, b_wait)
 
-            def x_wait(k):
+        def x_wait(k):
+            @pl.when(a_needed(f))
+            def _():
+                arrived(xd.at[f, chunk(k)], xdrecv.at[f, k])
+                forwards(f, k, start)
+
+            @pl.when(b_needed(f))
+            def _():
                 arrived(xa.at[f, chunk(k)], xarecv.at[f, k])
                 sideways(f, k, start)
 
-            span(CHUNKS, x_wait)
+        span(CHUNKS, x_wait)
+
+        @pl.when(a_needed(f))
+        def _():
+            s[...] -= dot(abuf[f], xd[f])
+
+        @pl.when(b_needed(f))
+        def _():
             s[...] -= dot(xa[f], bbuf[f])
 
     span(FRONTS, update)
@@ -384,18 +402,19 @@
 
             span(CHUNKS // 2, lambda at: spread(lowest + at, start))
 
-    store = pltpu.make_async_copy(s, out, loc.at[0])
-    store.start()
+    @pl.when(mine == 0)
+    def _():
+        span(FRONTS, lambda f: rest(f, start, start))
 
     @pl.when(mine == 0)
     def _():
         for f in range(FRONTS):
             factors(f, sent)
         for f in range(FRONTS - 1):
-            tiles(f, True, sent, nothing)
-
-    tiles(FRONTS - 1, True, sent, nothing)
-    span(FRONTS, lambda f: tiles(f, False, sent, nothing))
+            near(f, sent, nothing)
+
+    near(FRONTS - 1, sent, nothing)
+    span(FRONTS, lambda f: rest(f, sent, nothing))
 
     def drain(f):
         @pl.when(a_needed(f))
@@ -415,23 +434,22 @@
     @pl.when(solver)
     def _():
         span(CHUNKS, lambda k: spread(k, sent))
-
-    store.wait()
 
 
 def per_device(rows, cols, work, a, b, u, v, shift):
     first = max(0, (rows + cols) // 2 - FRONTS)
     width = work.shape[0]
     tile = (width, width)
-    any_ref = pl.BlockSpec(memory_space=pl.ANY)
+    hbm_ref = pl.BlockSpec(memory_space=pltpu.HBM)
+    work, a, b, u, v = (pltpu.with_memory_space_constraint(x, pltpu.HBM) for x in (work, a, b, u, v))
     dma = pltpu.SemaphoreType.DMA
     stack = [pltpu.VMEM((FRONTS,) + tile, BF)]
     return pl.pallas_call(
         functools.partial(kernel, rows, cols, first),
-        out_shape=jax.ShapeDtypeStruct(work.shape, work.dtype),
-        in_specs=[any_ref] * 5 + [pl.BlockSpec(memory_space=pltpu.SMEM)],
-        out_specs=any_ref,
-        scratch_shapes=[pltpu.VMEM(tile, F32)] * 3 + [pltpu.VMEM((5,) + tile, BF)] * 4
+        out_shape=pltpu.VMEM(work.shape, work.dtype),
+        in_specs=[hbm_ref] * 5 + [pl.BlockSpec(memory_space=pltpu.SMEM)],
+        out_specs=pl.BlockSpec(memory_space=pltpu.VMEM),
+        scratch_shapes=[pltpu.VMEM(tile, F32)] * 2 + [pltpu.VMEM((5,) + tile, BF)] * 4
         + [pltpu.VMEM((3,) + tile, BF)] * 2
         + [pltpu.VMEM(tile, BF)] + stack * 4
         + [dma((3,)), dma((FRONTS,)), dma((cols,)), dma((FRONTS,)), dma((rows,)),
@@ -440,7 +458,7 @@
            dma((CHUNKS, 2)), dma((CHUNKS, cols - 1)), dma((FRONTS, CHUNKS, 2)),
            dma((FRONTS, CHUNKS)), dma((FRONTS, CHUNKS)), dma((FRONTS, CHUNKS)), dma((2,)), dma((2,))],
         compiler_params=pltpu.CompilerParams(
-            collective_id=0, has_side_effects=True, vmem_limit_bytes=63 * 1024 * 1024),
+            collective_id=0, has_side_effects=True, vmem_limit_bytes=48 * 1024 * 1024),
     )(work, a, b, u, v, shift)
 
 

time: 72.5 us -> 70.7 us (0.975)
  the two profiles are of different devices: /device:TPU:20 before, /device:TPU:29 now
where the time goes in v4:
time: 70.7 us; the launch traced here: 70.5 us
  Pallas kernels  68.9 us (97%)
  local copies, waits for them, and re-layouts  0.97 us (1%)
    pallas_call x1, Pallas kernels, per_device(): pl.pallas_call(functools.partial(kernel, rows, cols, first), out_shape=pl...  68.9 us

profile of v4, /device:TPU:29, one launch (start us, length us, event | category | flops | bytes accessed | tf_op | source)
XLA Modules:
  0.0 70.5 jit_solution(13688584783091842960)
XLA Ops:
  0.7 68.9 %shard_map.64 = f32[512,512]{1,0:T(8,128)S(1)} custom-call(f32[512,512]{1,0:T(8,128)} %work.1, bf16[1,8,128,512]{3,2,1,0:T(8,128)(2,1)} %a.1, bf16[4,1,64,512]{3,2,1,0:T(8,128)(2,1)} %b.1, f32[1,3,128,512]{3,2,1,0:T(8,128)} %u.1, f32[1,3,64,512]{3,2,1,0:T(8,128)} %v.1, f32[1]{0:T(128)S(6)} %copy.9.shift), custom_call_target="tpu_custom_call" | custom-call | tf_op jit(solution)/shard_map/pallas_call | solution.py:447
  69.5 1.0 %copy.8 = f32[512,512]{1,0:T(8,128)} copy(f32[512,512]{1,0:T(8,128)S(1)} %shard_map.64) | data formatting | bytes 2097152

commit v5 on v4

--- a/solution.py
+++ b/solution.py
@@ -23,13 +23,23 @@
     return high, (value - high.astype(F32)).astype(BF)
 
 
-def product(left, right):
-    (lh, ll), (rh, rl) = left, right
-    return dot(lh, rh) + (dot(lh, rl) + dot(ll, rh))
+def lay_left(parts):
+    high, low = parts
+    return [high, high, low]
+
+
+def lay_right(parts):
+    high, low = parts
+    return [high, low, high]
+
+
+def product(lefts, rights):
+    left = jnp.concatenate(sum(map(lay_left, lefts), []), axis=1)
+    return dot(left, jnp.concatenate(sum(map(lay_right, rights), []), axis=0))
 
 
 def kernel(rows, cols, first, work, a, b, u, v, shift, s,
-           ubuf, vbuf, uh, ul, vh, vl, yh, yl, xs, abuf, bbuf, xd, xa,
+           ubuf, vbuf, utop, ulow, vnear, vfar, y, xs, abuf, bbuf, xd, xa,
            loc, usend, urecv, vsend, vrecv, asend, arecv, aloc, bsend, brecv, bloc,
            dsend, xsend, fsend, ssend, xdrecv, xarecv, vpass, vgot):
     r = lax.axis_index("row")
@@ -197,35 +207,44 @@
 
     t, e = slice(0, half), slice(half, width)
 
-    def prepare(high, low, buf, corner, scale):
-        x, y = corner
-
-        def put(slot, part, value):
-            high[(slot,) + part], low[(slot,) + part] = split(value)
-
-        def get(slot, part):
-            return high[(slot,) + part], low[(slot,) + part]
-
-        def square(slot, part):
-            if part != corner:
-                return product(get(slot, part), get(slot, part))
-            return (product(get(slot, (x, x)), get(slot, corner))
-                    + product(get(slot, corner), get(slot, (y, y))))
-
+    def prepare(buf, corner, scale, keep):
+        x, z = corner
         parts = ((t, t), (e, e), corner)
         eye = (lax.broadcasted_iota(jnp.int32, (half, half), 0)
                == lax.broadcasted_iota(jnp.int32, (half, half), 1)).astype(F32)
-        for part in parts:
-            put(4, part, buf[part])
-        for part in parts:
-            base = buf[part]
-            put(0, part, ((eye - base) if part != corner else -base) * scale)
-        for part in parts:
-            value = square(4, part)
-            put(2, part, value)
-            put(1, part, (buf[part] - value) * scale)
-        for part in parts:
-            put(3, part, square(2, part))
+
+        def squares(values):
+            both = [split(value) for value in values]
+            out = [product([both[at]], [both[at]]) for at in range(2)]
+            first_at, second_at = (0, 1) if x == t else (1, 0)
+            out.append(product([both[first_at], both[2]], [both[2], both[second_at]]))
+            return out, both
+
+        base = [buf[p, q] for p, q in parts]
+        second, _ = squares(base)
+        for at, part in enumerate(parts):
+            keep(0, at, split(((eye - base[at]) if at < 2 else -base[at]) * scale))
+            keep(1, at, split((base[at] - second[at]) * scale))
+        fourth, both = squares(second)
+        for at, part in enumerate(parts):
+            keep(2, at, both[at])
+            keep(3, at, split(fourth[at]))
+
+    def keep_u(slot, at, parts):
+        value = jnp.concatenate(lay_left(parts), axis=1)
+        if at == 0:
+            utop[slot] = value
+        else:
+            place = 3 * half * (2 - at)
+            ulow[slot, :, place:place + 3 * half] = value
+
+    def keep_v(slot, at, parts):
+        value = jnp.concatenate(lay_right(parts), axis=0)
+        if at == 0:
+            vnear[slot * 3 * half:(slot + 1) * 3 * half, :] = value
+        else:
+            place = (2 * slot + 2 - at) * 3 * half
+            vfar[place:place + 3 * half, :] = value
 
     @pl.when(solver)
     def _():
@@ -238,7 +257,7 @@
                 u_filled(at, lambda part: arrived(ubuf.at[place, part], urecv.at[at]))
 
         span(cols, u_wait)
-        prepare(uh, ul, ubuf, (e, t), 1.0)
+        prepare(ubuf, (e, t), 1.0, keep_u)
 
     @pl.when(mine == 0)
     def _():
@@ -274,7 +293,7 @@
 
     @pl.when(solver)
     def _():
-        prepare(vh, vl, vbuf, (t, e), 0.5 / jnp.broadcast_to(shift[0], (1, half)).astype(F32))
+        prepare(vbuf, (t, e), 0.5 / jnp.broadcast_to(shift[0], (1, half)).astype(F32), keep_v)
 
     def chunk(k):
         return pl.ds(pl.multiple_of(k * ch, ch), ch)
@@ -291,13 +310,18 @@
                 act(remote(part, part, fsend.at[f, k, 1], xdrecv.at[f, k], r + 2, c))
 
     square = cols == 4
+
+    def relays(f):
+        source = first + f - r
+        if not square:
+            return source < 0
+        return ((source == 0) & (c == 2)) | ((source == 1) & (c == 3) & (f == FRONTS - 1))
 
     def sideways(f, k, act):
         if square:
             part = xa.at[f, chunk(k)]
-            source = first + f - r
-
-            @pl.when(((source == 0) & (c == 2)) | ((source == 1) & (c == 3) & (f == FRONTS - 1)))
+
+            @pl.when(relays(f))
             def _():
                 act(remote(part, part, ssend.at[f, k], xarecv.at[f, k], r, 5 - c))
 
@@ -330,22 +354,28 @@
 
             span(rows, b_wait)
 
+        def d_wait(k):
+            arrived(xd.at[f, chunk(k)], xdrecv.at[f, k])
+            forwards(f, k, start)
+
         def x_wait(k):
-            @pl.when(a_needed(f))
-            def _():
-                arrived(xd.at[f, chunk(k)], xdrecv.at[f, k])
-                forwards(f, k, start)
-
-            @pl.when(b_needed(f))
-            def _():
-                arrived(xa.at[f, chunk(k)], xarecv.at[f, k])
-                sideways(f, k, start)
-
-        span(CHUNKS, x_wait)
+            arrived(xa.at[f, chunk(k)], xarecv.at[f, k])
+            sideways(f, k, start)
+
+        relay = b_needed(f) & relays(f)
+
+        @pl.when(relay)
+        def _():
+            span(CHUNKS, x_wait)
 
         @pl.when(a_needed(f))
         def _():
+            span(CHUNKS, d_wait)
             s[...] -= dot(abuf[f], xd[f])
+
+        @pl.when(b_needed(f) & jnp.logical_not(relay))
+        def _():
+            span(CHUNKS, x_wait)
 
         @pl.when(b_needed(f))
         def _():
@@ -376,26 +406,33 @@
 
     @pl.when(solver)
     def _():
-        for part, extent in ((t, half), (e, width)):
-            now = s[part, :]
-            yh[0, part, :], yl[0, part, :] = split(now)
+        def put(stage, at, value):
+            y[stage, at * 3 * half:(at + 1) * 3 * half, :] = jnp.concatenate(
+                lay_right(split(value)), axis=0)
+
+        for at, part in enumerate((t, e)):
+            put(0, at, s[part, :])
 
             def left(slot, stage):
-                return split(product((uh[slot, part, :extent], ul[slot, part, :extent]),
-                                     (yh[stage, :extent, :], yl[stage, :extent, :])))
+                if at == 0:
+                    moved = dot(utop[slot], y[stage, :3 * half, :])
+                else:
+                    moved = dot(ulow[slot], y[stage])
+                high, low = split(moved)
+                return lay_left((high[:, :half], low[:, :half])), lay_left((high[:, half:], low[:, half:]))
 
             def right(slot, moved):
-                high, low = moved
-                near = product((high[:, :half], low[:, :half]),
-                               (vh[slot, :half, :half], vl[slot, :half, :half]))
-                far = product((high, low), (vh[slot, :, half:], vl[slot, :, half:]))
-                return jnp.concatenate([near, far], axis=1)
-
-            zero, one = left(0, 0), left(1, 0)
-            now = right(0, zero) + right(1, one)
+                count = len(moved)
+                near_part = jnp.concatenate(sum((m[0] for m in moved), []), axis=1)
+                far_part = jnp.concatenate(sum((m[0] + m[1] for m in moved), []), axis=1)
+                left_half = dot(near_part, vnear[slot * 3 * half:(slot + count) * 3 * half, :])
+                right_half = dot(far_part, vfar[slot * 6 * half:(slot + count) * 6 * half, :])
+                return jnp.concatenate([left_half, right_half], axis=1)
+
+            now = right(0, [left(0, 0), left(1, 0)])
             for stage in (1, 2):
-                yh[stage, part, :], yl[stage, part, :] = split(now)
-                now = now + right(stage + 1, left(stage + 1, stage))
+                put(stage, at, now)
+                now = now + right(stage + 1, [left(stage + 1, stage)])
             s[part, :] = now
             xs[part, :] = now.astype(BF)
             lowest = part.start // ch
@@ -439,7 +476,7 @@
 def per_device(rows, cols, work, a, b, u, v, shift):
     first = max(0, (rows + cols) // 2 - FRONTS)
     width = work.shape[0]
-    tile = (width, width)
+    tile, half = (width, width), width // 2
     hbm_ref = pl.BlockSpec(memory_space=pltpu.HBM)
     work, a, b, u, v = (pltpu.with_memory_space_constraint(x, pltpu.HBM) for x in (work, a, b, u, v))
     dma = pltpu.SemaphoreType.DMA
@@ -449,8 +486,10 @@
         out_shape=pltpu.VMEM(work.shape, work.dtype),
         in_specs=[hbm_ref] * 5 + [pl.BlockSpec(memory_space=pltpu.SMEM)],
         out_specs=pl.BlockSpec(memory_space=pltpu.VMEM),
-        scratch_shapes=[pltpu.VMEM(tile, F32)] * 2 + [pltpu.VMEM((5,) + tile, BF)] * 4
-        + [pltpu.VMEM((3,) + tile, BF)] * 2
+        scratch_shapes=[pltpu.VMEM(tile, F32)] * 2 + [
+            pltpu.VMEM((4, half, 3 * half), BF), pltpu.VMEM((4, half, 6 * half), BF),
+            pltpu.VMEM((12 * half, half), BF), pltpu.VMEM((24 * half, half), BF),
+            pltpu.VMEM((3, 6 * half, width), BF)]
         + [pltpu.VMEM(tile, BF)] + stack * 4
         + [dma((3,)), dma((FRONTS,)), dma((cols,)), dma((FRONTS,)), dma((rows,)),
            dma((FRONTS, cols)), dma((FRONTS, cols)), dma((FRONTS,)),

time: 70.7 us -> 66.2 us (0.936)
  the two profiles are of different devices: /device:TPU:29 before, /device:TPU:31 now
where the time goes in v5:
time: 66.2 us; the launch traced here: 66 us
  Pallas kernels  64.4 us (97%)
  local copies, waits for them, and re-layouts  0.97 us (1%)
    pallas_call x1, Pallas kernels, per_device(): pl.pallas_call(functools.partial(kernel, rows, cols, first), out_shape=pl...  64.4 us

profile of v5, /device:TPU:31, one launch (start us, length us, event | category | flops | bytes accessed | tf_op | source)
XLA Modules:
  0.0 66.0 jit_solution(15590583431432007998)
XLA Ops:
  0.7 64.4 %shard_map.64 = f32[512,512]{1,0:T(8,128)S(1)} custom-call(f32[512,512]{1,0:T(8,128)} %work.1, bf16[1,8,128,512]{3,2,1,0:T(8,128)(2,1)} %a.1, bf16[4,1,64,512]{3,2,1,0:T(8,128)(2,1)} %b.1, f32[1,3,128,512]{3,2,1,0:T(8,128)} %u.1, f32[1,3,64,512]{3,2,1,0:T(8,128)} %v.1, f32[1]{0:T(128)S(6)} %copy.9.shift), custom_call_target="tpu_custom_call" | custom-call | tf_op jit(solution)/shard_map/pallas_call | solution.py:484
  65.0 1.0 %copy.8 = f32[512,512]{1,0:T(8,128)} copy(f32[512,512]{1,0:T(8,128)S(1)} %shard_map.64) | data formatting | bytes 2097152

commit v6 on v5

--- a/solution.py
+++ b/solution.py
@@ -39,7 +39,7 @@
 
 
 def kernel(rows, cols, first, work, a, b, u, v, shift, s,
-           ubuf, vbuf, utop, ulow, vnear, vfar, y, xs, abuf, bbuf, xd, xa,
+           ubuf, vbuf, utop, ulow, vnear, vfar, y, begun, xs, abuf, bbuf, xd, xa,
            loc, usend, urecv, vsend, vrecv, asend, arecv, aloc, bsend, brecv, bloc,
            dsend, xsend, fsend, ssend, xdrecv, xarecv, vpass, vgot):
     r = lax.axis_index("row")
@@ -259,9 +259,29 @@
         span(cols, u_wait)
         prepare(ubuf, (e, t), 1.0, keep_u)
 
+    def put(stage, at, value):
+        y[stage, at * 3 * half:(at + 1) * 3 * half, :] = jnp.concatenate(
+            lay_right(split(value)), axis=0)
+
+    def left(at, slot, stage):
+        if at == 0:
+            moved = dot(utop[slot], y[stage, :3 * half, :])
+        else:
+            moved = dot(ulow[slot], y[stage])
+        high, low = split(moved)
+        return jnp.concatenate(lay_left((high[:, :half], low[:, :half]))
+                               + lay_left((high[:, half:], low[:, half:])), axis=1)
+
+    def begin(at):
+        put(0, at, s[(t, e)[at], :])
+        begun[at, :, :6 * half] = left(at, 0, 0)
+        begun[at, :, 6 * half:] = left(at, 1, 0)
+
     @pl.when(mine == 0)
     def _():
         send_ahead(False)
+        begin(0)
+        begin(1)
 
     beside = jnp.where(even, r + 1, r - 1)
     passing = solver & (mine != 1) & ((mine == 0) == even)
@@ -315,7 +335,9 @@
         source = first + f - r
         if not square:
             return source < 0
-        return ((source == 0) & (c == 2)) | ((source == 1) & (c == 3) & (f == FRONTS - 1))
+        final = f == FRONTS - 1
+        onward = (c == 2) & ((source == 0) | ((source == 1) & jnp.logical_not(final)))
+        return onward | ((c == 3) & (source == 1) & final)
 
     def sideways(f, k, act):
         if square:
@@ -367,6 +389,7 @@
         @pl.when(relay)
         def _():
             span(CHUNKS, x_wait)
+            s[...] -= dot(xa[f], bbuf[f])
 
         @pl.when(a_needed(f))
         def _():
@@ -376,12 +399,15 @@
         @pl.when(b_needed(f) & jnp.logical_not(relay))
         def _():
             span(CHUNKS, x_wait)
-
-        @pl.when(b_needed(f))
-        def _():
             s[...] -= dot(xa[f], bbuf[f])
 
     span(FRONTS, update)
+
+    held = (c == 0) & (mine == 0) & square
+
+    def spread_held(k, act):
+        if square:
+            act(remote(xs.at[chunk(k)], xa.at[mine, chunk(k)], xsend.at[k, 1], xarecv.at[mine, k], r, 2))
 
     def spread(k, act):
         part = xs.at[chunk(k)]
@@ -392,7 +418,9 @@
             act(remote(part, there, dsend.at[k, 0], xdrecv.at[mine, k], r + 1, c))
 
         def right(at):
-            relayed = (c == 0) & (at == 3) | (c == 1) & (at == 1) & last if square else at < 0
+            relayed = at < 0
+            if square:
+                relayed = ((c == 0) & (at == 3)) | ((c == 1) & (at == jnp.where(last, 1, 2))) | (held & (at == 2))
 
             @pl.when((c + at < cols) & jnp.logical_not(relayed))
             def _():
@@ -406,33 +434,22 @@
 
     @pl.when(solver)
     def _():
-        def put(stage, at, value):
-            y[stage, at * 3 * half:(at + 1) * 3 * half, :] = jnp.concatenate(
-                lay_right(split(value)), axis=0)
-
         for at, part in enumerate((t, e)):
-            put(0, at, s[part, :])
-
-            def left(slot, stage):
-                if at == 0:
-                    moved = dot(utop[slot], y[stage, :3 * half, :])
-                else:
-                    moved = dot(ulow[slot], y[stage])
-                high, low = split(moved)
-                return lay_left((high[:, :half], low[:, :half])), lay_left((high[:, half:], low[:, half:]))
-
-            def right(slot, moved):
-                count = len(moved)
-                near_part = jnp.concatenate(sum((m[0] for m in moved), []), axis=1)
-                far_part = jnp.concatenate(sum((m[0] + m[1] for m in moved), []), axis=1)
-                left_half = dot(near_part, vnear[slot * 3 * half:(slot + count) * 3 * half, :])
-                right_half = dot(far_part, vfar[slot * 6 * half:(slot + count) * 6 * half, :])
+            @pl.when(mine != 0)
+            def _():
+                begin(at)
+
+            def right(slot, count, moved):
+                left_half = dot(jnp.concatenate([m[:, :3 * half] for m in moved], axis=1),
+                                vnear[slot * 3 * half:(slot + count) * 3 * half, :])
+                right_half = dot(jnp.concatenate(moved, axis=1) if count > 1 else moved[0],
+                                 vfar[slot * 6 * half:(slot + count) * 6 * half, :])
                 return jnp.concatenate([left_half, right_half], axis=1)
 
-            now = right(0, [left(0, 0), left(1, 0)])
+            now = right(0, 2, [begun[at, :, :6 * half], begun[at, :, 6 * half:]])
             for stage in (1, 2):
                 put(stage, at, now)
-                now = now + right(stage + 1, [left(stage + 1, stage)])
+                now = now + right(stage + 1, 1, [left(at, stage + 1, stage)])
             s[part, :] = now
             xs[part, :] = now.astype(BF)
             lowest = part.start // ch
@@ -442,6 +459,11 @@
     @pl.when(mine == 0)
     def _():
         span(FRONTS, lambda f: rest(f, start, start))
+
+    @pl.when(held)
+    def _():
+        span(CHUNKS, lambda k: spread(k, sent))
+        span(CHUNKS, lambda k: spread_held(k, start))
 
     @pl.when(mine == 0)
     def _():
@@ -468,7 +490,11 @@
     def _():
         pass_v(sent)
 
-    @pl.when(solver)
+    @pl.when(held)
+    def _():
+        span(CHUNKS, lambda k: spread_held(k, sent))
+
+    @pl.when(solver & jnp.logical_not(held))
     def _():
         span(CHUNKS, lambda k: spread(k, sent))
 
@@ -489,7 +515,7 @@
         scratch_shapes=[pltpu.VMEM(tile, F32)] * 2 + [
             pltpu.VMEM((4, half, 3 * half), BF), pltpu.VMEM((4, half, 6 * half), BF),
             pltpu.VMEM((12 * half, half), BF), pltpu.VMEM((24 * half, half), BF),
-            pltpu.VMEM((3, 6 * half, width), BF)]
+            pltpu.VMEM((3, 6 * half, width), BF), pltpu.VMEM((2, half, 12 * half), BF)]
         + [pltpu.VMEM(tile, BF)] + stack * 4
         + [dma((3,)), dma((FRONTS,)), dma((cols,)), dma((FRONTS,)), dma((rows,)),
            dma((FRONTS, cols)), dma((FRONTS, cols)), dma((FRONTS,)),

time: 66.2 us -> 72.9 us (1.10)
  Pallas kernels: 64.4 us -> 71.1 us
    pallas_call x1, Pallas kernels: 64.4 us -> 71.1 us  [per_device(): pl.pallas_call(functools.partial(kernel, rows, cols, first), out_shape=pl...]
where the time goes in v6:
time: 72.9 us; the launch traced here: 72.7 us
  Pallas kernels  71.1 us (98%)
  local copies, waits for them, and re-layouts  0.97 us (1%)
    pallas_call x1, Pallas kernels, per_device(): pl.pallas_call(functools.partial(kernel, rows, cols, first), out_shape=pl...  71.1 us

profile of v6, /device:TPU:31, one launch (start us, length us, event | category | flops | bytes accessed | tf_op | source)
XLA Modules:
  0.0 72.7 jit_solution(11545582095260957649)
XLA Ops:
  0.7 71.1 %shard_map.64 = f32[512,512]{1,0:T(8,128)S(1)} custom-call(f32[512,512]{1,0:T(8,128)} %work.1, bf16[1,8,128,512]{3,2,1,0:T(8,128)(2,1)} %a.1, bf16[4,1,64,512]{3,2,1,0:T(8,128)(2,1)} %b.1, f32[1,3,128,512]{3,2,1,0:T(8,128)} %u.1, f32[1,3,64,512]{3,2,1,0:T(8,128)} %v.1, f32[1]{0:T(128)S(6)} %copy.9.shift), custom_call_target="tpu_custom_call" | custom-call | tf_op jit(solution)/shard_map/pallas_call | solution.py:510
  71.8 1.0 %copy.8 = f32[512,512]{1,0:T(8,128)} copy(f32[512,512]{1,0:T(8,128)S(1)} %shard_map.64) | data formatting | bytes 2097152

commit v7 on v5

--- a/solution.py
+++ b/solution.py
@@ -301,13 +301,9 @@
     def forwards(f, k, act):
         part = xd.at[f, chunk(k)]
 
-        @pl.when(even)
-        def _():
-            act(remote(part, part, fsend.at[f, k, 0], xdrecv.at[f, k], r + 1, c))
-
-            @pl.when(r + 2 < rows)
-            def _():
-                act(remote(part, part, fsend.at[f, k, 1], xdrecv.at[f, k], r + 2, c))
+        @pl.when(r + 1 < rows)
+        def _():
+            act(remote(part, part, fsend.at[f, k], xdrecv.at[f, k], r + 1, c))
 
     square = cols == 4
 
@@ -383,26 +379,32 @@
 
     span(FRONTS, update)
 
+    def across(k, at, act):
+        relayed = at < 0
+        if square:
+            relayed = ((c == 0) & (at == 3)) | ((c == 1) & (at == 1) & last)
+
+        @pl.when((c + at < cols) & jnp.logical_not(relayed))
+        def _():
+            act(remote(xs.at[chunk(k)], xa.at[mine, chunk(k)], xsend.at[k, at - 1],
+                       xarecv.at[mine, k], r, c + at))
+
     def spread(k, act):
-        part = xs.at[chunk(k)]
-        there, across = xd.at[mine, chunk(k)], xa.at[mine, chunk(k)]
-
         @pl.when(r + 1 < rows)
         def _():
-            act(remote(part, there, dsend.at[k, 0], xdrecv.at[mine, k], r + 1, c))
-
-        def right(at):
-            relayed = (c == 0) & (at == 3) | (c == 1) & (at == 1) & last if square else at < 0
-
-            @pl.when((c + at < cols) & jnp.logical_not(relayed))
-            def _():
-                act(remote(part, across, xsend.at[k, at - 1], xarecv.at[mine, k], r, c + at))
-
-        span(cols - 1, lambda at: right(at + 1))
-
-        @pl.when(even & (r + 2 < rows))
-        def _():
-            act(remote(part, there, dsend.at[k, 1], xdrecv.at[mine, k], r + 2, c))
+            act(remote(xs.at[chunk(k)], xd.at[mine, chunk(k)], dsend.at[k],
+                       xdrecv.at[mine, k], r + 1, c))
+
+        across(k, 1, act)
+
+        @pl.when(last)
+        def _():
+            span(cols - 2, lambda at: across(k, at + 2, act))
+
+    def spread_late(act):
+        @pl.when(solver & jnp.logical_not(last))
+        def _():
+            span(cols - 2, lambda at: span(CHUNKS, lambda k: across(k, at + 2, act)))
 
     @pl.when(solver)
     def _():
@@ -439,6 +441,8 @@
 
             span(CHUNKS // 2, lambda at: spread(lowest + at, start))
 
+    spread_late(start)
+
     @pl.when(mine == 0)
     def _():
         span(FRONTS, lambda f: rest(f, start, start))
@@ -471,6 +475,8 @@
     @pl.when(solver)
     def _():
         span(CHUNKS, lambda k: spread(k, sent))
+
+    spread_late(sent)
 
 
 def per_device(rows, cols, work, a, b, u, v, shift):
@@ -494,7 +500,7 @@
         + [dma((3,)), dma((FRONTS,)), dma((cols,)), dma((FRONTS,)), dma((rows,)),
            dma((FRONTS, cols)), dma((FRONTS, cols)), dma((FRONTS,)),
            dma((FRONTS, cols)), dma((FRONTS, rows)), dma((FRONTS,)),
-           dma((CHUNKS, 2)), dma((CHUNKS, cols - 1)), dma((FRONTS, CHUNKS, 2)),
+           dma((CHUNKS,)), dma((CHUNKS, cols - 1)), dma((FRONTS, CHUNKS)),
            dma((FRONTS, CHUNKS)), dma((FRONTS, CHUNKS)), dma((FRONTS, CHUNKS)), dma((2,)), dma((2,))],
         compiler_params=pltpu.CompilerParams(
             collective_id=0, has_side_effects=True, vmem_limit_bytes=48 * 1024 * 1024),

time: 66.2 us -> 69 us (1.042)
  Pallas kernels: 64.4 us -> 67.2 us
    pallas_call x1, Pallas kernels: 64.4 us -> 67.2 us  [per_device(): pl.pallas_call(functools.partial(kernel, rows, cols, first), out_shape=pl...]
where the time goes in v7:
time: 69 us; the launch traced here: 68.8 us
  Pallas kernels  67.2 us (97%)
  local copies, waits for them, and re-layouts  0.97 us (1%)
    pallas_call x1, Pallas kernels, per_device(): pl.pallas_call(functools.partial(kernel, rows, cols, first), out_shape=pl...  67.2 us

profile of v7, /device:TPU:31, one launch (start us, length us, event | category | flops | bytes accessed | tf_op | source)
XLA Modules:
  0.0 68.8 jit_solution(10194955130846522232)
XLA Ops:
  0.7 67.2 %shard_map.64 = f32[512,512]{1,0:T(8,128)S(1)} custom-call(f32[512,512]{1,0:T(8,128)} %work.1, bf16[1,8,128,512]{3,2,1,0:T(8,128)(2,1)} %a.1, bf16[4,1,64,512]{3,2,1,0:T(8,128)(2,1)} %b.1, f32[1,3,128,512]{3,2,1,0:T(8,128)} %u.1, f32[1,3,64,512]{3,2,1,0:T(8,128)} %v.1, f32[1]{0:T(128)S(6)} %copy.9.shift), custom_call_target="tpu_custom_call" | custom-call | tf_op jit(solution)/shard_map/pallas_call | solution.py:490
  67.8 1.0 %copy.8 = f32[512,512]{1,0:T(8,128)} copy(f32[512,512]{1,0:T(8,128)S(1)} %shard_map.64) | data formatting | bytes 2097152

commit v8 on v7

--- a/solution.py
+++ b/solution.py
@@ -311,7 +311,7 @@
         source = first + f - r
         if not square:
             return source < 0
-        return ((source == 0) & (c == 2)) | ((source == 1) & (c == 3) & (f == FRONTS - 1))
+        return (((source == 0) & (c == 2)) | ((source == 1) & (c == 3))) & (f == FRONTS - 1)
 
     def sideways(f, k, act):
         if square:
@@ -382,7 +382,7 @@
     def across(k, at, act):
         relayed = at < 0
         if square:
-            relayed = ((c == 0) & (at == 3)) | ((c == 1) & (at == 1) & last)
+            relayed = (((c == 0) & (at == 3)) | ((c == 1) & (at == 1))) & last
 
         @pl.when((c + at < cols) & jnp.logical_not(relayed))
         def _():

time: 69 us -> 72.4 us (1.049)
  Pallas kernels: 67.2 us -> 70.6 us
    pallas_call x1, Pallas kernels: 67.2 us -> 70.6 us  [per_device(): pl.pallas_call(functools.partial(kernel, rows, cols, first), out_shape=pl...]
where the time goes in v8:
time: 72.4 us; the launch traced here: 72.2 us
  Pallas kernels  70.6 us (98%)
  local copies, waits for them, and re-layouts  0.97 us (1%)
    pallas_call x1, Pallas kernels, per_device(): pl.pallas_call(functools.partial(kernel, rows, cols, first), out_shape=pl...  70.6 us

profile of v8, /device:TPU:31, one launch (start us, length us, event | category | flops | bytes accessed | tf_op | source)
XLA Modules:
  0.0 72.2 jit_solution(10877357862542550057)
XLA Ops:
  0.7 70.6 %shard_map.64 = f32[512,512]{1,0:T(8,128)S(1)} custom-call(f32[512,512]{1,0:T(8,128)} %work.1, bf16[1,8,128,512]{3,2,1,0:T(8,128)(2,1)} %a.1, bf16[4,1,64,512]{3,2,1,0:T(8,128)(2,1)} %b.1, f32[1,3,128,512]{3,2,1,0:T(8,128)} %u.1, f32[1,3,64,512]{3,2,1,0:T(8,128)} %v.1, f32[1]{0:T(128)S(6)} %copy.9.shift), custom_call_target="tpu_custom_call" | custom-call | tf_op jit(solution)/shard_map/pallas_call | solution.py:490
  71.2 1.0 %copy.8 = f32[512,512]{1,0:T(8,128)} copy(f32[512,512]{1,0:T(8,128)S(1)} %shard_map.64) | data formatting | bytes 2097152
